TPU v7x, 256 devices: a whole 4x4x8 slice. The times are simulated.
256 devices in a mesh: file: 2 (over x_hi), seq: 32 (over y, z), tp: 4 (over x_lo, core).
Axes of the slice: x: 4 (x_hi: 2, x_lo: 2; x = x_hi * 2 + x_lo), y: 4, z: 8, core: 2. Of those that a mesh axis runs over, the one named last changes fastest.
Arguments:
- queries: bfloat16 [32768, 4096], P(('file', 'tp', 'seq')), parts along dimension 0
- keys: bfloat16 [32768, 1024], P(('file', 'tp', 'seq')), parts along dimension 0
- values: bfloat16 [32768, 1024], P(('file', 'tp', 'seq')), parts along dimension 0, may hold values from -6 to 6
- mem_pos: int32 [2048], P(('file', 'tp', 'seq')), parts along dimension 0, may hold values from 0 to 16383, as said below
- norm_gain: float32 [4096], replicated, may hold values from 0.1 to 1.9
- summary_weight: bfloat16 [4096, 6144], P('tp', 'seq'), may hold values from -0.09375 to 0.09375
Outputs:
- encoded: bfloat16 [32768, 4096], P(('file', 'tp', 'seq')), parts along dimension 0
- summary: bfloat16 [2048, 6144], P(('file', 'tp'), 'seq'), parts along dimension 0
There are 2 independent parts, one for each index of `file`. A program takes and returns all parts, laid end to end along the dimension named above; an argument that names none is the same for every part. Nothing has to cross between parts.
Inputs may be any that keep to these rules, and one draw needn't show every extreme that they name: `mem_pos`: entry j lies among rows 16 * j to 16 * j + 15.
All inputs are finite; a program needn't handle non-finite values.
Results may differ from a plain program's by a relative error of at most 0.018.
Values may be sent and summed in bfloat16 or wider, within the bound.
No kernel may reach another device: no remote copies, remote signals or barrier semaphores. Data moves between devices by JAX's collectives and lax.ppermute only.
A program may use at most 64 MiB of HBM per device.

v0:
```python
import jax
import jax.numpy as jnp
from jax import lax
from jax.sharding import PartitionSpec as P

D = 4096
HEADS = 32
KV_HEADS = 8
HEAD_DIM = 128


def from_behind(block, axis, distance):
    devices = range(lax.axis_size(axis))
    route = [(i - distance, i) for i in devices if i - distance in devices]
    return lax.ppermute(block, axis, route)


def widen(packed):
    count = packed.shape[0]
    group = HEADS // KV_HEADS
    spread = jnp.broadcast_to(
        packed.reshape(count, KV_HEADS, 1, HEAD_DIM), (count, KV_HEADS, group, HEAD_DIM)
    )
    return spread.reshape(count, HEADS * HEAD_DIM)


def on_device(queries, keys, values, mem_pos, norm_gain, summary_weight):
    rows = queries.shape[0]
    n_seq = lax.axis_size("seq")
    n_tp = lax.axis_size("tp")
    heads_dev = HEADS // n_seq
    scale = 1.0 / HEAD_DIM**0.5
    span = rows * n_seq
    block = 512
    blocks = span // block
    shifted = from_behind(jnp.stack((keys, values)), "tp", 1)
    moved_q, moved_k, moved_v, prior_k, prior_v = (
        lax.all_to_all(queries, "seq", split_axis=1, concat_axis=0, tiled=True),
        lax.all_to_all(widen(keys), "seq", split_axis=1, concat_axis=0, tiled=True),
        lax.all_to_all(widen(values), "seq", split_axis=1, concat_axis=0, tiled=True),
        lax.all_to_all(widen(shifted[0]), "seq", split_axis=1, concat_axis=0, tiled=True),
        lax.all_to_all(widen(shifted[1]), "seq", split_axis=1, concat_axis=0, tiled=True),
    )
    query_heads = moved_q.reshape(span, heads_dev, HEAD_DIM)
    keys_all = jnp.concatenate((prior_k, moved_k), axis=0)
    values_all = jnp.concatenate((prior_v, moved_v), axis=0)
    has_prior = lax.axis_index("tp") > 0

    def one_block(qb):
        q_first = qb * block
        q_block = lax.dynamic_slice_in_dim(query_heads, q_first, block, 0)
        q_where = q_first + jnp.arange(block, dtype=jnp.int32)

        def step(index, state):
            peak, total, accum = state
            k_first = q_first + index * block
            key_block = lax.dynamic_slice_in_dim(keys_all, k_first, block, 0).reshape(
                block, heads_dev, HEAD_DIM
            )
            value_block = lax.dynamic_slice_in_dim(values_all, k_first, block, 0).reshape(
                block, heads_dev, HEAD_DIM
            )
            k_where = k_first + jnp.arange(block, dtype=jnp.int32)
            seen = (k_where[None, :] > q_where[:, None]) & (
                k_where[None, :] <= q_where[:, None] + span
            )
            seen = seen & ((k_where >= span) | has_prior)[None, :]
            scores = (
                jnp.einsum("qhd,khd->qhk", q_block, key_block, preferred_element_type=jnp.float32)
                * scale
            )
            masked = jnp.where(seen[:, None, :], scores, -jnp.inf)
            newest = jnp.maximum(peak, jnp.max(masked, axis=2))
            fade = jnp.exp(peak - newest)
            weights = jnp.where(seen[:, None, :], jnp.exp(scores - newest[:, :, None]), 0.0)
            total = total * fade + jnp.sum(weights, axis=2)
            accum = accum * fade[:, :, None] + jnp.einsum(
                "qhk,khd->qhd",
                weights.astype(jnp.bfloat16),
                value_block,
                preferred_element_type=jnp.float32,
            )
            return (newest, total, accum)

        start_state = (
            jnp.full((block, heads_dev), -1e30, jnp.float32),
            jnp.zeros((block, heads_dev), jnp.float32),
            jnp.zeros((block, heads_dev, HEAD_DIM), jnp.float32),
        )
        peak, total, accum = lax.fori_loop(0, blocks + 1, step, start_state)
        return accum / total[:, :, None]

    pieces = lax.map(one_block, jnp.arange(blocks, dtype=jnp.int32))
    attended = pieces.reshape(span, heads_dev * HEAD_DIM).astype(jnp.bfloat16)
    encoded = lax.all_to_all(attended, "seq", split_axis=0, concat_axis=1, tiled=True)
    local_rows = mem_pos % rows
    picked = jnp.take(encoded, local_rows, axis=0).astype(jnp.float32)
    meansq = jnp.mean(picked * picked, axis=1, keepdims=True)
    normed = (picked * lax.rsqrt(meansq + 1e-05) * norm_gain[None, :]).astype(jnp.bfloat16)
    mem_dev = normed.shape[0]
    width = D // n_tp
    memory_full = lax.all_gather(normed, ("seq", "tp"), axis=0, tiled=True)
    ordered = jnp.transpose(memory_full.reshape(n_seq, n_tp, mem_dev, D), (1, 0, 2, 3)).reshape(
        n_tp * n_seq * mem_dev, D
    )
    memory_mine = lax.dynamic_slice_in_dim(ordered, lax.axis_index("tp") * width, width, 1)
    summary = lax.psum_scatter(
        jnp.dot(memory_mine, summary_weight, preferred_element_type=jnp.float32).astype(
            jnp.bfloat16
        ),
        "tp",
        scatter_dimension=0,
        tiled=True,
    )
    return (encoded, summary)


def solution(mesh):
    placed = (
        P(("file", "tp", "seq"), None),
        P(("file", "tp", "seq"), None),
        P(("file", "tp", "seq"), None),
        P(("file", "tp", "seq")),
        P(),
        P("tp", "seq"),
    )
    return jax.shard_map(
        on_device,
        mesh=mesh,
        in_specs=placed,
        out_specs=(P(("file", "tp", "seq"), None), P(("file", "tp"), "seq")),
        check_vma=False,
    )
```

profile of v0, /device:TPU:4, one launch (start us, length us, event | category | flops | bytes accessed | tf_op | source)
XLA Modules:
  0.0 749.5 jit_solution(9203760285174816247)
XLA Ops:
  9.5 11.5 %all-to-all-start.4 = ((bf16[128,32,128]{2,0,1:T(8,128)(2,1)}), bf16[128,32,128]{2,0,1:T(8,128)(2,1)S(1)}, u32[]{:S(2)}, u32[]{:S(2)}) async-start(bf16[128,32,128]{2,0,1:T(8,128)(2,1)} %bitcast.17), calls=%async_computation.4 | async-start | bytes 2097152 | tf_op jit(solution)/shard_map/all_to_all | solution.py:40
  21.0 28.6 %all-to-all-done.4 = bf16[128,32,128]{2,0,1:T(8,128)(2,1)S(1)} async-done(((bf16[128,32,128]{2,0,1:T(8,128)(2,1)}), bf16[128,32,128]{2,0,1:T(8,128)(2,1)S(1)}, u32[]{:S(2)}, u32[]{:S(2)}) %all-to-all-start.4) | async-done | bytes 1048608 | tf_op jit(solution)/shard_map/all_to_all | solution.py:40
  50.8 5.1 all-to-all-start.2
  57.2 27.0 %all-to-all-done.2 = bf16[128,32,128]{2,0,1:T(8,128)(2,1)S(1)} async-done(((bf16[128,32,128]{2,0,1:T(8,128)(2,1)}), bf16[128,32,128]{2,0,1:T(8,128)(2,1)S(1)}, u32[]{:S(2)}, u32[]{:S(2)}) %all-to-all-start.2) | async-done | bytes 1048608 | tf_op jit(solution)/shard_map/all_to_all | solution.py:39
  84.2 4.9 all-to-all-start
  94.6 22.9 %all-to-all-done = bf16[128,32,128]{0,2,1:T(8,128)(2,1)S(1)} async-done(((bf16[128,32,128]{0,2,1:T(8,128)(2,1)}), bf16[128,32,128]{0,2,1:T(8,128)(2,1)S(1)}, u32[]{:S(2)}, u32[]{:S(2)}) %all-to-all-start) | async-done | bytes 1048608 | tf_op jit(solution)/shard_map/all_to_all | solution.py:38
  117.4 2.2 broadcast_in_dim.92
  119.6 5.0 all-to-all-start.3
  126.4 26.5 %all-to-all-done.3 = bf16[128,32,128]{2,0,1:T(8,128)(2,1)} async-done(((bf16[128,32,128]{2,0,1:T(8,128)(2,1)}), bf16[128,32,128]{2,0,1:T(8,128)(2,1)}, u32[]{:S(2)}, u32[]{:S(2)}) %all-to-all-start.3) | async-done | bytes 1048608 | tf_op jit(solution)/shard_map/all_to_all | solution.py:42
  152.9 2.2 broadcast_in_dim.88
  155.1 5.0 all-to-all-start.1
  161.5 2.7 pad_maximum_fusion.1
  164.2 24.2 %all-to-all-done.1 = bf16[128,32,128]{2,0,1:T(8,128)(2,1)} async-done(((bf16[128,32,128]{2,0,1:T(8,128)(2,1)}), bf16[128,32,128]{2,0,1:T(8,128)(2,1)}, u32[]{:S(2)}, u32[]{:S(2)}) %all-to-all-start.1) | async-done | bytes 1048608 | tf_op jit(solution)/shard_map/all_to_all | solution.py:41
  188.4 2.7 pad_maximum_fusion
  191.1 271.2 %while.31 = (s32[]{:T(128)}, bf16[8,512,1,128]{3,1,0,2:T(8,128)(2,1)}, s32[8]{0:T(128)S(1)}, bf16[4096,1,128]{2,0,1:T(8,128)(2,1)}, pred[]{:T(512)}, /*index=5*/...) while((s32[]{:T(128)}, ...), condition=%wide.region_5.6_spmd, body=%wide.region_0.5_spmd.sunk | while | flops 140056064 | bytes 5304871 | solution.py:93
  193.3 30.9 %while.32 = (s32[]{:T(128)}, f32[512,1]{0,1:T(1,128)S(1)}, f32[512,1]{0,1:T(1,128)S(1)}, f32[512,1,128]{0,2,1:T(8,128)S(1)}, s32[]{:T(128)}, /*index=5*/pred[]{:...) while((s32[]{:T(128)}, f32[512,1]{0,1:T(1,128)S(1)}, ...), condition=%wide.region_4.4_spmd.clone.clone.clone, body=%wide.region_1.3_spmd.clone.clone.clone.sunk | while | flops 139924992 | bytes 4122848 | solution.py:90
  227.2 30.9 %while.32 = (s32[]{:T(128)}, f32[512,1]{0,1:T(1,128)S(1)}, f32[512,1]{0,1:T(1,128)S(1)}, f32[512,1,128]{0,2,1:T(8,128)S(1)}, s32[]{:T(128)}, /*index=5*/pred[]{:...) while((s32[]{:T(128)}, f32[512,1]{0,1:T(1,128)S(1)}, ...), condition=%wide.region_4.4_spmd.clone.clone.clone, body=%wide.region_1.3_spmd.clone.clone.clone.sunk | while | flops 139924992 | bytes 4122848 | solution.py:90
  236.0 1.5 fusion.44
  261.1 30.9 %while.32 = (s32[]{:T(128)}, f32[512,1]{0,1:T(1,128)S(1)}, f32[512,1]{0,1:T(1,128)S(1)}, f32[512,1,128]{0,2,1:T(8,128)S(1)}, s32[]{:T(128)}, /*index=5*/pred[]{:...) while((s32[]{:T(128)}, f32[512,1]{0,1:T(1,128)S(1)}, ...), condition=%wide.region_4.4_spmd.clone.clone.clone, body=%wide.region_1.3_spmd.clone.clone.clone.sunk | while | flops 139924992 | bytes 4122848 | solution.py:90
  269.9 1.5 fusion.44
  295.0 30.9 %while.32 = (s32[]{:T(128)}, f32[512,1]{0,1:T(1,128)S(1)}, f32[512,1]{0,1:T(1,128)S(1)}, f32[512,1,128]{0,2,1:T(8,128)S(1)}, s32[]{:T(128)}, /*index=5*/pred[]{:...) while((s32[]{:T(128)}, f32[512,1]{0,1:T(1,128)S(1)}, ...), condition=%wide.region_4.4_spmd.clone.clone.clone, body=%wide.region_1.3_spmd.clone.clone.clone.sunk | while | flops 139924992 | bytes 4122848 | solution.py:90
  300.3 1.5 fusion.44
  303.8 1.5 fusion.44
  310.6 1.5 fusion.44
  328.9 30.9 %while.32 = (s32[]{:T(128)}, f32[512,1]{0,1:T(1,128)S(1)}, f32[512,1]{0,1:T(1,128)S(1)}, f32[512,1,128]{0,2,1:T(8,128)S(1)}, s32[]{:T(128)}, /*index=5*/pred[]{:...) while((s32[]{:T(128)}, f32[512,1]{0,1:T(1,128)S(1)}, ...), condition=%wide.region_4.4_spmd.clone.clone.clone, body=%wide.region_1.3_spmd.clone.clone.clone.sunk | while | flops 139924992 | bytes 4122848 | solution.py:90
  334.2 1.5 fusion.44
  337.7 1.5 fusion.44
  344.5 1.5 fusion.44
  354.8 1.5 fusion.44
  362.8 30.9 %while.32 = (s32[]{:T(128)}, f32[512,1]{0,1:T(1,128)S(1)}, f32[512,1]{0,1:T(1,128)S(1)}, f32[512,1,128]{0,2,1:T(8,128)S(1)}, s32[]{:T(128)}, /*index=5*/pred[]{:...) while((s32[]{:T(128)}, f32[512,1]{0,1:T(1,128)S(1)}, ...), condition=%wide.region_4.4_spmd.clone.clone.clone, body=%wide.region_1.3_spmd.clone.clone.clone.sunk | while | flops 139924992 | bytes 4122848 | solution.py:90
  368.1 1.5 fusion.44
  378.4 1.5 fusion.44
  385.3 1.5 fusion.44
  388.7 1.5 fusion.44
  396.7 30.9 %while.32 = (s32[]{:T(128)}, f32[512,1]{0,1:T(1,128)S(1)}, f32[512,1]{0,1:T(1,128)S(1)}, f32[512,1,128]{0,2,1:T(8,128)S(1)}, s32[]{:T(128)}, /*index=5*/pred[]{:...) while((s32[]{:T(128)}, f32[512,1]{0,1:T(1,128)S(1)}, ...), condition=%wide.region_4.4_spmd.clone.clone.clone, body=%wide.region_1.3_spmd.clone.clone.clone.sunk | while | flops 139924992 | bytes 4122848 | solution.py:90
  402.0 1.5 fusion.44
  412.3 1.5 fusion.44
  419.2 1.5 fusion.44
  422.6 1.5 fusion.44
  430.6 30.9 %while.32 = (s32[]{:T(128)}, f32[512,1]{0,1:T(1,128)S(1)}, f32[512,1]{0,1:T(1,128)S(1)}, f32[512,1,128]{0,2,1:T(8,128)S(1)}, s32[]{:T(128)}, /*index=5*/pred[]{:...) while((s32[]{:T(128)}, f32[512,1]{0,1:T(1,128)S(1)}, ...), condition=%wide.region_4.4_spmd.clone.clone.clone, body=%wide.region_1.3_spmd.clone.clone.clone.sunk | while | flops 139924992 | bytes 4122848 | solution.py:90
  453.1 1.5 fusion.44
  456.5 1.5 fusion.44
  462.3 5.0 all-to-all-start.5
  467.4 28.2 %all-to-all-done.5 = bf16[32,128,128]{2,1,0:T(8,128)(2,1)S(1)} async-done(((bf16[32,128,128]{2,1,0:T(8,128)(2,1)}), bf16[32,128,128]{2,1,0:T(8,128)(2,1)S(1)}, u32[]{:S(2)}, u32[]{:S(2)}) %all-to-all-start.5) | async-done | bytes 1048608 | tf_op jit(solution)/shard_map/all_to_all | solution.py:95
  497.4 216.7 %all-gather.2.cloned.1.call-done = bf16[1024,4096]{1,0:T(8,128)(2,1)} async-done(((bf16[8,4096]{1,0:T(8,128)(2,1)}), bf16[1024,4096]{1,0:T(8,128)(2,1)}) %all-gather.2.cloned.1.call-update) | async-done | bytes 8388624 | tf_op jit(solution)/shard_map/all_gather | solution.py:102
  714.2 7.7 %copy.28 = bf16[32,4,8,4096]{3,2,0,1:T(8,128)(2,1)} copy(bf16[32,4,8,4096]{3,2,1,0:T(8,128)(2,1)} %bitcast.99) | data formatting | bytes 16777216 | tf_op jit(solution)/shard_map/reshape | solution.py:103
  721.9 3.2 fusion.21
  725.1 17.6 %reduce-scatter.2.cloned.1.call-done = bf16[256,192]{0,1:T(8,128)(2,1)} async-done(((bf16[1024,192]{0,1:T(8,128)(2,1)}), bf16[256,192]{0,1:T(8,128)(2,1)}) %reduce-scatter.2.cloned.1.call-update) | async-done | bytes 98320 | tf_op jit(solution)/shard_map/reduce_scatter | solution.py:107
  (732 shorter events, 246.7 us)
Async XLA Ops:
  7.2 714.7 %copy-start = (bf16[1024,192]{0,1:T(8,128)(2,1)S(1)}, bf16[1024,192]{0,1:T(8,128)(2,1)}, u32[]{:S(2)}) copy-start(bf16[1024,192]{0,1:T(8,128)(2,1)} %param.15) | copy-start | bytes 1179652
  7.2 13.8 %copy-start.3 = (bf16[128,1024]{1,0:T(8,128)(2,1)S(1)}, bf16[128,1024]{1,0:T(8,128)(2,1)}, u32[]{:S(2)}) copy-start(bf16[128,1024]{1,0:T(8,128)(2,1)} %param.11) | copy-start | bytes 786436
  9.5 40.1 %all-to-all-start.4 = ((bf16[128,32,128]{2,0,1:T(8,128)(2,1)}), bf16[128,32,128]{2,0,1:T(8,128)(2,1)S(1)}, u32[]{:S(2)}, u32[]{:S(2)}) async-start(bf16[128,32,128]{2,0,1:T(8,128)(2,1)} %bitcast.17), calls=%async_computation.4 | async-start | bytes 2097152 | tf_op jit(solution)/shard_map/all_to_all | solution.py:40
  21.0 34.9 %copy-start.2 = (bf16[128,4096]{1,0:T(8,128)(2,1)S(1)}, bf16[128,4096]{1,0:T(8,128)(2,1)}, u32[]{:S(2)}) copy-start(bf16[128,4096]{1,0:T(8,128)(2,1)} %param.10) | copy-start | bytes 3145732
  50.8 33.4 %all-to-all-start.2 = ((bf16[128,32,128]{2,0,1:T(8,128)(2,1)}), bf16[128,32,128]{2,0,1:T(8,128)(2,1)S(1)}, u32[]{:S(2)}, u32[]{:S(2)}) async-start(bf16[128,32,128]{2,0,1:T(8,128)(2,1)} %bitcast.11), calls=%async_computation.2 | async-start | bytes 2097152 | tf_op jit(solution)/shard_map/all_to_all | solution.py:39
  84.2 33.2 %all-to-all-start = ((bf16[128,32,128]{0,2,1:T(8,128)(2,1)}), bf16[128,32,128]{0,2,1:T(8,128)(2,1)S(1)}, u32[]{:S(2)}, u32[]{:S(2)}) async-start(bf16[128,32,128]{0,2,1:T(8,128)(2,1)} %bitcast.3), calls=%async_computation | async-start | bytes 2097152 | tf_op jit(solution)/shard_map/all_to_all | solution.py:38
  90.2 2.8 collective-permute-start
  119.6 33.3 %all-to-all-start.3 = ((bf16[128,32,128]{2,0,1:T(8,128)(2,1)}), bf16[128,32,128]{2,0,1:T(8,128)(2,1)}, u32[]{:S(2)}, u32[]{:S(2)}) async-start(bf16[128,32,128]{2,0,1:T(8,128)(2,1)} %bitcast.14), calls=%async_computation.3 | async-start | bytes 2097152 | tf_op jit(solution)/shard_map/all_to_all | solution.py:42
  155.1 33.3 %all-to-all-start.1 = ((bf16[128,32,128]{2,0,1:T(8,128)(2,1)}), bf16[128,32,128]{2,0,1:T(8,128)(2,1)}, u32[]{:S(2)}, u32[]{:S(2)}) async-start(bf16[128,32,128]{2,0,1:T(8,128)(2,1)} %bitcast.8), calls=%async_computation.1 | async-start | bytes 2097152 | tf_op jit(solution)/shard_map/all_to_all | solution.py:41
  462.3 5.1 copy-start.5
  462.3 34.3 %copy-start.4 = (f32[4096]{0:T(1024)S(1)}, f32[4096]{0:T(1024)}, u32[]{:S(2)}) copy-start(f32[4096]{0:T(1024)} %param.14) | copy-start | bytes 49156
  462.3 33.3 %all-to-all-start.5 = ((bf16[32,128,128]{2,1,0:T(8,128)(2,1)}), bf16[32,128,128]{2,1,0:T(8,128)(2,1)S(1)}, u32[]{:S(2)}, u32[]{:S(2)}) async-start(bf16[32,128,128]{2,1,0:T(8,128)(2,1)} %bitcast.20), calls=%async_computation.5 | async-start | bytes 2097152 | tf_op jit(solution)/shard_map/all_to_all | solution.py:95
  467.3 246.8 %all-gather.2.cloned.1.call-start = ((), (), s32[]{:S(2)}) async-start(), calls=%async_computation.7 | async-start | bytes 8454144 | tf_op jit(solution)/shard_map/all_gather | solution.py:102
  495.8 226.1 %copy-start.1 = (bf16[128,4096]{1,0:T(8,128)(2,1)}, bf16[128,4096]{1,0:T(8,128)(2,1)S(1)}, u32[]{:S(2)}) copy-start(bf16[128,4096]{1,0:T(8,128)(2,1)S(1)} %copy_bitcast_fusion) | copy-start | bytes 3145732
  497.4 245.3 %reduce-scatter.2.cloned.1.call-start = ((), (), s32[]{:S(2)}) async-start(), calls=%async_computation.8 | async-start | bytes 491520 | tf_op jit(solution)/shard_map/reduce_scatter | solution.py:107
Sparse Core Ops, SparseCore 0:
  497.5 216.6 all-gather.1
  725.2 17.4 reduce-scatter.1
where the time goes:
time: 755 us; the launch traced here: 750 us
  waiting for transfers between devices  393 us (52%)
  matrix products  210 us (28%)
  other arithmetic  42.5 us (6%)
  local copies, waits for them, and re-layouts  40.9 us (5%)
  starting transfers between devices  37.9 us (5%)
  between operations  14.2 us (2%)
  loops' own time  11 us (1%)
    all_gather x1, waiting for transfers between devices, on_device(): memory_full = lax.all_gather(normed, ('seq', 'tp'), axis=0, tiled=True)  217 us
    dot_general x72, matrix products, step(): jnp.einsum('qhk,khd->qhd', weights.astype(jnp.bfloat16), value_block, pre...  108 us
    dot_general x72, matrix products, step(): jnp.einsum('qhd,khd->qhk', q_block, key_block, preferred_element_type=jnp...  98.1 us
    reduce_sum x72, other arithmetic, step(): total = total * fade + jnp.sum(weights, axis=2)  31.3 us
    all_to_all x1, waiting for transfers between devices, on_device(): lax.all_to_all(widen(values), 'seq', split_axis=1, concat_axis=0, tiled=T...  28.6 us
    all_to_all x1, waiting for transfers between devices, on_device(): lax.all_to_all(attended, 'seq', split_axis=0, concat_axis=1, tiled=True)  28.2 us
    all_to_all x1, waiting for transfers between devices, on_device(): lax.all_to_all(widen(keys), 'seq', split_axis=1, concat_axis=0, tiled=True)  27 us
    all_to_all x1, waiting for transfers between devices, on_device(): lax.all_to_all(widen(shifted[1]), 'seq', split_axis=1, concat_axis=0, til...  26.5 us
  transfers between devices with their start and end apart: 9, of which 9 were waited for; matrix products, arithmetic and copies ran while one was open for 1% of the time, Pallas kernels for 0%

commit v1 on v0

v1 whole, which is shorter than its diff:
```python
import functools

import jax
import jax.numpy as jnp
from jax import lax
from jax.experimental import pallas as pl
from jax.experimental.pallas import tpu as pltpu
from jax.sharding import Mesh, PartitionSpec as P

D = 4096
HEADS = 32
KV_HEADS = 8
HEAD_DIM = 128
GROUP_HEADS = HEADS // KV_HEADS
ROWS = 128
N_Z = 8
N_Y = 4
SPAN = ROWS * N_Z
WINDOW = 4096
PRIOR = WINDOW // SPAN
TILE = 256
CHUNK = 512
CALLS = 2
COEF = 1.4426950408889634 / HEAD_DIM**0.5
PLACES = ("y", "xl", "core")
GROUPS = 4 * N_Y


def scores_of(q, k):
    return lax.dot_general(q, k, (((1,), (1,)), ((), ())), preferred_element_type=jnp.float32)


def mix(p, v):
    return jnp.dot(p, v, preferred_element_type=jnp.float32)


def attend_kernel(heads, absent_ref, q_ref, *refs):
    pieces, (o_ref, k_all, v_all, q_rows) = refs[: PRIOR + 1], refs[PRIOR + 1 :]
    step = pl.program_id(0)
    blocks = TILE // ROWS
    count = heads * TILE

    @pl.when(step == 0)
    def _():
        for slot, piece in enumerate(pieces):
            for z in range(N_Z):
                at = pl.ds(slot * SPAN + z * ROWS, ROWS)
                k_all[at, :] = piece[z, 0]
                v_all[at, :HEAD_DIM] = piece[z, 1]
                v_all[at, HEAD_DIM:] = jnp.ones((ROWS, HEAD_DIM), jnp.bfloat16)
        absent = absent_ref[0]
        for slot in range(PRIOR):

            @pl.when(slot < absent)
            def _():
                first = k_all[pl.ds(pl.multiple_of(absent * SPAN, SPAN), 16), :][:1, :]
                at = pl.ds(slot * SPAN, SPAN)
                k_all[at, :] = jnp.broadcast_to(first, (SPAN, HEAD_DIM))
                v_all[at, :] = jnp.zeros((SPAN, 2 * HEAD_DIM), jnp.bfloat16)

    for h in range(heads):
        for b in range(blocks):
            q_rows[h * TILE + b * ROWS : h * TILE + (b + 1) * ROWS, :] = q_ref[
                b, :, h * HEAD_DIM : (h + 1) * HEAD_DIM
            ]
    q = q_rows[...]
    start = step * TILE

    def window(ref, offset, size):
        return ref[pl.ds(pl.multiple_of(start + offset, TILE), size), :]

    row = lax.broadcasted_iota(jnp.int32, (1, TILE, TILE), 1)
    col = lax.broadcasted_iota(jnp.int32, (1, TILE, TILE), 2)
    own = col <= row
    oldest = scores_of(q, window(k_all, 0, TILE)).reshape(heads, TILE, TILE)
    newest = scores_of(q, window(k_all, WINDOW, TILE)).reshape(heads, TILE, TILE)
    s = jnp.where(own, newest, oldest).reshape(count, TILE)
    peak = jnp.max(s, axis=1, keepdims=True)
    p = jnp.exp2(s * COEF - peak * COEF).astype(jnp.bfloat16).reshape(heads, TILE, TILE)
    zero = jnp.zeros((), jnp.bfloat16)
    total = mix(jnp.where(own, p, zero).reshape(count, TILE), window(v_all, WINDOW, TILE))
    total += mix(jnp.where(own, zero, p).reshape(count, TILE), window(v_all, 0, TILE))
    offset = TILE
    while offset < WINDOW:
        size = min(CHUNK, WINDOW - offset)
        s = scores_of(q, window(k_all, offset, size))
        higher = jnp.maximum(peak, jnp.max(s, axis=1, keepdims=True))
        fade = jnp.exp2(peak * COEF - higher * COEF)
        p = jnp.exp2(s * COEF - higher * COEF).astype(jnp.bfloat16)
        total = total * fade + mix(p, window(v_all, offset, size))
        peak = higher
        offset += size
    out = (total[:, :HEAD_DIM] / total[:, HEAD_DIM:]).astype(jnp.bfloat16)
    for h in range(heads):
        for b in range(blocks):
            o_ref[b, :, h * HEAD_DIM : (h + 1) * HEAD_DIM] = out[
                h * TILE + b * ROWS : h * TILE + (b + 1) * ROWS, :
            ]


def attend(q, pieces, absent):
    heads = q.shape[2] // HEAD_DIM
    blocks = TILE // ROWS
    rows = pl.BlockSpec((blocks, ROWS, heads * HEAD_DIM), lambda i, a: (i, 0, 0))
    whole = pl.BlockSpec((N_Z, 2, ROWS, HEAD_DIM), lambda i, a: (0, 0, 0, 0))
    return pl.pallas_call(
        functools.partial(attend_kernel, heads),
        grid_spec=pltpu.PrefetchScalarGridSpec(
            num_scalar_prefetch=1,
            grid=(SPAN // TILE,),
            in_specs=[rows] + [whole] * (PRIOR + 1),
            out_specs=rows,
            scratch_shapes=[
                pltpu.VMEM((WINDOW + SPAN, HEAD_DIM), jnp.bfloat16),
                pltpu.VMEM((WINDOW + SPAN, 2 * HEAD_DIM), jnp.bfloat16),
                pltpu.VMEM((heads * TILE, HEAD_DIM), jnp.bfloat16),
            ],
        ),
        out_shape=jax.ShapeDtypeStruct(q.shape, q.dtype),
        compiler_params=pltpu.CompilerParams(vmem_limit_bytes=48 * 2**20),
        cost_estimate=pl.CostEstimate(
            flops=heads * SPAN * WINDOW * HEAD_DIM * 8,
            bytes_accessed=4 * 2**20,
            transcendentals=heads * SPAN * WINDOW,
        ),
    )(absent, q, *pieces)


def to_groups(a, axis="z"):
    return lax.all_to_all(a, axis, split_axis=0, concat_axis=0, tiled=True)


def from_group_behind(a, back):
    def index(group):
        return group % N_Y * (GROUPS // N_Y) + group // N_Y

    return lax.ppermute(a, PLACES, [(index(g - back), index(g)) for g in range(back, GROUPS)])


def on_device(queries, keys, values, mem_pos, norm_gain, summary_weight):
    xl, core, y = lax.axis_index("xl"), lax.axis_index("core"), lax.axis_index("y")
    place = (xl * 2 + core) * N_Y + y

    packed = jnp.stack(
        (keys.reshape(ROWS, KV_HEADS, HEAD_DIM), values.reshape(ROWS, KV_HEADS, HEAD_DIM))
    )
    own = to_groups(jnp.transpose(packed, (2, 0, 1, 3)))
    pieces = [from_group_behind(own, back) for back in range(PRIOR, 0, -1)] + [own]
    absent = jnp.maximum(PRIOR - place, 0).astype(jnp.int32).reshape(1)

    heads = GROUP_HEADS // CALLS
    by_group = jnp.transpose(
        queries.reshape(ROWS, N_Z, CALLS, heads * HEAD_DIM), (2, 1, 0, 3)
    )
    q_parts = [to_groups(by_group[c]) for c in range(CALLS)]

    w_y = [summary_weight] + [
        lax.ppermute(summary_weight, "y", [(i, (i + s) % N_Y) for i in range(N_Y)])
        for s in range(1, N_Y)
    ]
    w_y = jnp.stack(w_y)
    w_x = jnp.stack((w_y, lax.ppermute(w_y, "xl", [(0, 1), (1, 0)])))
    w_all = jnp.stack((w_x, lax.ppermute(w_x, "core", [(0, 1), (1, 0)])))

    sent = [to_groups(attend(q, pieces, absent)) for q in q_parts]
    encoded = jnp.transpose(jnp.stack(sent), (2, 1, 0, 3)).reshape(ROWS, D)

    picked = jnp.take(encoded, mem_pos % ROWS, axis=0).astype(jnp.float32)
    meansq = jnp.mean(picked * picked, axis=1, keepdims=True)
    normed = (picked * lax.rsqrt(meansq + 1e-05) * norm_gain[None, :]).astype(jnp.bfloat16)
    mem_dev = normed.shape[0]
    memory = to_groups(jnp.broadcast_to(normed[None], (N_Z, mem_dev, D)))
    memory = memory.reshape(N_Z * mem_dev, 2, 2, D // 4)
    sums = 0.0
    for c in range(2):
        for x in range(2):
            part = lax.dynamic_slice(
                memory, (0, (xl + x) % 2, (core + c) % 2, 0), (N_Z * mem_dev, 1, 1, D // 4)
            ).reshape(N_Z * mem_dev, D // 4)
            sums += jnp.einsum(
                "rk,ykn->yrn", part, w_all[c, x], preferred_element_type=jnp.float32
            )
    sums = jnp.take(sums.astype(jnp.bfloat16), (y - jnp.arange(N_Y)) % N_Y, axis=0)
    summary = to_groups(sums, "y").reshape(N_Y * N_Z * mem_dev, -1)
    return encoded, summary


def solution(mesh):
    split = Mesh(mesh.devices.reshape(-1, N_Y, N_Z, 2, 2), ("file", "y", "z", "xl", "core"))
    tokens = ("file", "xl", "core", "y", "z")
    return jax.shard_map(
        on_device,
        mesh=split,
        in_specs=(
            P(tokens, None),
            P(tokens, None),
            P(tokens, None),
            P(tokens),
            P(),
            P(("xl", "core"), ("y", "z")),
        ),
        out_specs=(P(tokens, None), P(("file", "xl", "core"), ("y", "z"))),
        check_vma=False,
    )
```

time: 755 us -> 183 us (0.24)
  the two profiles are of different devices: /device:TPU:4 before, /device:TPU:2 now
where the time goes in v1:
time: 183 us; the launch traced here: 182 us
  starting transfers between devices  61.7 us (34%)
  waiting for transfers between devices  53.3 us (29%)
  Pallas kernels  29.4 us (16%)
  local copies, waits for them, and re-layouts  11.1 us (6%)
  other arithmetic  10.5 us (6%)
  blocking collectives  8.36 us (5%)
  matrix products  6.87 us (4%)
    all_to_all x6, waiting for transfers between devices, to_groups(): return lax.all_to_all(a, axis, split_axis=0, concat_axis=0, tiled=True)  45.6 us
    all_to_all x6, starting transfers between devices, to_groups(): return lax.all_to_all(a, axis, split_axis=0, concat_axis=0, tiled=True)  33.5 us
    pallas_call x2, Pallas kernels, attend(): pl.pallas_call(functools.partial(attend_kernel, heads), grid_spec=pltpu.P...  29.4 us
    ppermute x4, starting transfers between devices, from_group_behind(): lax.ppermute(a, PLACES, [(index(g - back), index(g)) for g in range(back,...  23.5 us
    all_to_all x1, blocking collectives, to_groups(): return lax.all_to_all(a, axis, split_axis=0, concat_axis=0, tiled=True)  8.36 us
    ppermute x3, waiting for transfers between devices, on_device(): lax.ppermute(summary_weight, 'y', [(i, (i + s) % N_Y) for i in range(N_Y)])  7.25 us
    dot_general x4, matrix products, on_device(): jnp.einsum('rk,ykn->yrn', part, w_all[c, x], preferred_element_type=jnp.f...  6.87 us
    unnamed x19, local copies, waits for them, and re-layouts  5.05 us
  transfers between devices with their start and end apart: 15, of which 6 were waited for; matrix products, arithmetic and copies ran while one was open for 10% of the time, Pallas kernels for 16%

profile of v1, /device:TPU:2, one launch (start us, length us, event | category | flops | bytes accessed | tf_op | source)
XLA Modules:
  0.0 182.3 jit_solution(12351614237282039559)
XLA Ops:
  0.6 1.1 copy.22
  1.8 0.2 copy.24
  2.0 1.2 copy.21
  3.2 0.2 copy.23
  3.4 0.9 maximum_bitcast_fusion.1
  4.2 8.5 %all-to-all-start.1 = ((bf16[8,2,128,128]{3,2,1,0:T(8,128)(2,1)}), bf16[8,2,128,128]{3,2,1,0:T(8,128)(2,1)S(1)}, u32[]{:S(2)}, u32[]{:S(2)}) async-start(bf16[8,2,128,128]{3,2,1,0:T(8,128)(2,1)} %maximum_bitcast_fusion.1), calls=%async_computation.1 | async-start | bytes 1048576 | tf_op jit(solution)/shard_map/all_to_all | solution.py:130
  12.7 0.7 copy.19
  13.4 0.5 copy.20
  13.9 1.1 slice_bitcast_fusion.19
  15.0 15.2 %all-to-all-done.1.refs_4_ = bf16[8,2,128,128]{3,2,1,0:T(8,128)(2,1)S(1)} async-done(((bf16[8,2,128,128]{3,2,1,0:T(8,128)(2,1)}), bf16[8,2,128,128]{3,2,1,0:T(8,128)(2,1)S(1)}, u32[]{:S(2)}, u32[]{:S(2)}) %all-to-all-start.1) | async-done | bytes 524320 | tf_op jit(solution)/shard_map/all_to_all | solution.py:130
  30.2 3.5 %all-to-all-start.3 = ((bf16[8,128,256]{2,1,0:T(8,128)(2,1)}), bf16[8,128,256]{2,1,0:T(8,128)(2,1)S(1)}, u32[]{:S(2)}, u32[]{:S(2)}) async-start(bf16[8,128,256]{2,1,0:T(8,128)(2,1)} %get-tuple-element.15), calls=%async_computation.3 | async-start | bytes 1048576 | tf_op jit(solution)/shard_map/all_to_all | solution.py:130
  33.7 3.1 %collective-permute-start.6 = (bf16[1024,192]{0,1:T(8,128)(2,1)S(1)}, bf16[1024,192]{0,1:T(8,128)(2,1)}, u32[]{:S(2)}, u32[]{:S(2)}) collective-permute-start(bf16[1024,192]{0,1:T(8,128)(2,1)S(1)} %copy-done.3), channel_id=1, source_target_pairs={{0,96},{32,0},{64,32},{96,64},{1,97},{33,1},{65,33},{97,65},{2,98}... | collective-permute-start | bytes 1179656 | tf_op jit(solution)/shard_map/ppermute | solution.py:158
  36.8 0.6 collective-permute-start.5
  37.4 1.0 collective-permute-start.4
  38.4 1.9 %collective-permute-start = (bf16[8,2,128,128]{3,2,1,0:T(8,128)(2,1)S(1)}, bf16[8,2,128,128]{3,2,1,0:T(8,128)(2,1)S(1)}, u32[]{:S(2)}, u32[]{:S(2)}) collective-permute-start(bf16[8,2,128,128]{3,2,1,0:T(8,128)(2,1)S(1)} %all-to-all-done.1.refs_4_), channel_id=1, source_target_pairs={{0,1},{32,33},{64,65},{96,97},{1,2},{33,34},{65,66},{97,98},{2,3},... | collective-permute-start | bytes 1572872 | tf_op jit(solution)/shard_map/ppermute | solution.py:137
  40.3 4.2 %collective-permute-start.1 = (bf16[8,2,128,128]{3,2,1,0:T(8,128)(2,1)S(1)}, bf16[8,2,128,128]{3,2,1,0:T(8,128)(2,1)S(1)}, u32[]{:S(2)}, u32[]{:S(2)}) collective-permute-start(bf16[8,2,128,128]{3,2,1,0:T(8,128)(2,1)S(1)} %all-to-all-done.1.refs_4_), channel_id=1, source_target_pairs={{0,96},{32,1},{64,33},{96,65},{1,97},{33,2},{65,34},{97,66},{2,98}... | collective-permute-start | bytes 1572872 | tf_op jit(solution)/shard_map/ppermute | solution.py:137
  44.5 7.2 %collective-permute-done.6 = bf16[1024,192]{0,1:T(8,128)(2,1)} collective-permute-done((bf16[1024,192]{0,1:T(8,128)(2,1)S(1)}, bf16[1024,192]{0,1:T(8,128)(2,1)}, u32[]{:S(2)}, u32[]{:S(2)}) %collective-permute-start.6) | collective-permute-done | bytes 393248 | tf_op jit(solution)/shard_map/ppermute | solution.py:158
  51.7 1.9 %collective-permute-start.2 = (bf16[8,2,128,128]{3,2,1,0:T(8,128)(2,1)S(1)}, bf16[8,2,128,128]{3,2,1,0:T(8,128)(2,1)S(1)}, u32[]{:S(2)}, u32[]{:S(2)}) collective-permute-start(bf16[8,2,128,128]{3,2,1,0:T(8,128)(2,1)S(1)} %all-to-all-done.1.refs_4_), channel_id=1, source_target_pairs={{0,64},{32,96},{64,1},{96,33},{1,65},{33,97},{65,2},{97,34},{2,66}... | collective-permute-start | bytes 1572872 | tf_op jit(solution)/shard_map/ppermute | solution.py:137
  53.7 0.8 copy-done.4
  54.4 15.5 %collective-permute-start.3 = (bf16[8,2,128,128]{3,2,1,0:T(8,128)(2,1)S(1)}, bf16[8,2,128,128]{3,2,1,0:T(8,128)(2,1)}, u32[]{:S(2)}, u32[]{:S(2)}) collective-permute-start(bf16[8,2,128,128]{3,2,1,0:T(8,128)(2,1)S(1)} %all-to-all-done.1.refs_4_), channel_id=1, source_target_pairs={{0,32},{32,64},{64,96},{96,1},{1,33},{33,65},{65,97},{97,2},{2,34}... | collective-permute-start | bytes 1572872 | tf_op jit(solution)/shard_map/ppermute | solution.py:137
  70.0 6.8 %all-to-all-start = ((bf16[8,128,256]{2,1,0:T(8,128)(2,1)}), bf16[8,128,256]{2,1,0:T(8,128)(2,1)S(1)}, u32[]{:S(2)}, u32[]{:S(2)}) async-start(bf16[8,128,256]{2,1,0:T(8,128)(2,1)} %get-tuple-element.14), calls=%async_computation | async-start | bytes 1048576 | tf_op jit(solution)/shard_map/all_to_all | solution.py:130
  76.8 3.2 %fusion.25 = (bf16[1,4,1024,192]{2,3,1,0:T(8,128)(2,1)}, bf16[4,1024,192]{1,2,0:T(8,128)(2,1)}) fusion(bf16[1,1024,192]{1,2,0:T(8,128)(2,1)} %bitcast.15, bf16[1,1024,192]{1,2,0:T(8,128)(2,1)} %bitcast.73, bf16[1,1024,192]{1,2,0:T(8,128)(2,1)} %bitcast.13, bf16[1,1024,192]{1,2,0:T(8,128)(2,1)S(1)} %bitcast.72), kind=kLoop, calls=%fused_computation.62 | loop fusion | flops 2359296 | bytes 4718592 | tf_op jit(solution)/shard_map/stack | solution.py:162
  80.0 0.4 collective-permute-done.3.refs_3_
  80.4 14.7 %shard_map.78 = bf16[8,128,256]{2,1,0:T(8,128)(2,1)} custom-call(s32[1]{0:T(128)} %bitcast.absent_ref, bf16[8,128,256]{2,1,0:T(8,128)(2,1)S(1)} %all-to-all-done.3.q_ref, bf16[8,2,128,128]{3,2,1,0:T(8,128)(2,1)S(1)} %collective-permute-done.refs_0_, bf16[8,2,128,128]{3,2,1,0:T(8,128)(2,1)S(1)} %collective-permute-done.1.refs_1_, ...), custom_call_target="tpu_custom_call" | custom-call | flops 8589934592 | bytes 4194304 | tf_op jit(solution)/shard_map/pallas_call | solution.py:106
  95.1 6.8 %all-to-all-start.4 = ((bf16[8,128,256]{2,1,0:T(8,128)(2,1)}), bf16[8,128,256]{2,1,0:T(8,128)(2,1)}, u32[]{:S(2)}, u32[]{:S(2)}) async-start(bf16[8,128,256]{2,1,0:T(8,128)(2,1)} %shard_map.78), calls=%async_computation.4 | async-start | bytes 1048576 | tf_op jit(solution)/shard_map/all_to_all | solution.py:130
  101.9 14.7 %shard_map.77 = bf16[8,128,256]{2,1,0:T(8,128)(2,1)} custom-call(s32[1]{0:T(128)} %bitcast.absent_ref, bf16[8,128,256]{2,1,0:T(8,128)(2,1)S(1)} %all-to-all-done.q_ref, bf16[8,2,128,128]{3,2,1,0:T(8,128)(2,1)S(1)} %collective-permute-done.refs_0_, bf16[8,2,128,128]{3,2,1,0:T(8,128)(2,1)S(1)} %collective-permute-done.1.refs_1_, ...), custom_call_target="tpu_custom_call" | custom-call | flops 8589934592 | bytes 4194304 | tf_op jit(solution)/shard_map/pallas_call | solution.py:106
  116.6 2.7 %all-to-all-done.4 = bf16[8,128,256]{2,1,0:T(8,128)(2,1)} async-done(((bf16[8,128,256]{2,1,0:T(8,128)(2,1)}), bf16[8,128,256]{2,1,0:T(8,128)(2,1)}, u32[]{:S(2)}, u32[]{:S(2)}) %all-to-all-start.4) | async-done | bytes 524320 | tf_op jit(solution)/shard_map/all_to_all | solution.py:130
  119.3 4.5 %all-to-all-start.2 = ((bf16[8,128,256]{2,1,0:T(8,128)(2,1)}), bf16[8,128,256]{2,1,0:T(8,128)(2,1)S(1)}, u32[]{:S(2)}, u32[]{:S(2)}) async-start(bf16[8,128,256]{2,1,0:T(8,128)(2,1)} %shard_map.77), calls=%async_computation.2 | async-start | bytes 1048576 | tf_op jit(solution)/shard_map/all_to_all | solution.py:130
  123.8 4.9 %fusion.24 = (bf16[1,2,4,1024,192]{3,4,2,1,0:T(8,128)(2,1)}, bf16[2,4,1024,192]{2,3,1,0:T(8,128)(2,1)}) fusion(bf16[1,4,1024,192]{2,3,1,0:T(8,128)(2,1)} %bitcast.17, bf16[1,4,1024,192]{2,3,1,0:T(8,128)(2,1)} %get-tuple-element.12), kind=kLoop, calls=%fused_computation.61 | loop fusion | flops 1572864 | bytes 9437184 | tf_op jit(solution)/shard_map/stack | solution.py:163
  128.7 11.9 %all-to-all-done.2 = bf16[8,128,256]{2,1,0:T(8,128)(2,1)S(1)} async-done(((bf16[8,128,256]{2,1,0:T(8,128)(2,1)}), bf16[8,128,256]{2,1,0:T(8,128)(2,1)S(1)}, u32[]{:S(2)}, u32[]{:S(2)}) %all-to-all-start.2) | async-done | bytes 524320 | tf_op jit(solution)/shard_map/all_to_all | solution.py:130
  140.6 1.1 maximum_bitcast_fusion
  141.7 0.7 copy.25
  142.4 0.5 copy.27
  142.9 0.6 gather_fusion
  143.5 0.2 fusion.9
  143.8 0.1 fusion.11
  143.9 0.8 broadcast_in_dim.34
  144.7 3.5 %all-to-all-start.5 = ((bf16[8,8,4096]{2,1,0:T(8,128)(2,1)}), bf16[8,8,4096]{2,1,0:T(8,128)(2,1)S(1)}, u32[]{:S(2)}, u32[]{:S(2)}) async-start(bf16[8,8,4096]{2,1,0:T(8,128)(2,1)} %broadcast_in_dim.34), calls=%async_computation.5 | async-start | bytes 1048576 | tf_op jit(solution)/shard_map/all_to_all | solution.py:130
  148.3 15.8 %all-to-all-done.5 = bf16[8,8,4096]{2,1,0:T(8,128)(2,1)S(1)} async-done(((bf16[8,8,4096]{2,1,0:T(8,128)(2,1)}), bf16[8,8,4096]{2,1,0:T(8,128)(2,1)S(1)}, u32[]{:S(2)}, u32[]{:S(2)}) %all-to-all-start.5) | async-done | bytes 524320 | tf_op jit(solution)/shard_map/all_to_all | solution.py:130
  164.1 0.4 reshape.145
  164.5 1.1 constant_dynamic-slice_fusion.3
  165.6 2.0 %fusion.2 = f32[4,192,64]{1,2,0:T(8,128)S(1)} fusion(bf16[1,2,4,1024,192]{3,4,2,1,0:T(8,128)(2,1)} %get-tuple-element.10, bf16[64,1,1,1024]{3,2,1,0:T(2,128)(2,1)S(1)} %get-tuple-element.19), kind=kOutput, calls=%fused_computation.8 | convolution fusion | flops 100663296 | bytes 1900544 | tf_op jit(solution)/shard_map/rk,ykn->yrn/dot_general | solution.py:180
  167.7 2.2 %fusion = f32[4,192,64]{1,2,0:T(8,128)S(1)} fusion(bf16[1,2,4,1024,192]{3,4,2,1,0:T(8,128)(2,1)} %bitcast.21, bf16[64,1,1,1024]{3,2,1,0:T(2,128)(2,1)S(1)} %get-tuple-element.17), kind=kOutput, calls=%fused_computation.4 | convolution fusion | flops 100663296 | bytes 1900544 | tf_op jit(solution)/shard_map/rk,ykn->yrn/dot_general | solution.py:180
  169.8 2.0 %fusion.1 = f32[4,192,64]{1,2,0:T(8,128)S(1)} fusion(bf16[1,2,4,1024,192]{3,4,2,1,0:T(8,128)(2,1)} %bitcast.21, bf16[64,1,1,1024]{3,2,1,0:T(2,128)(2,1)S(1)} %get-tuple-element.18), kind=kOutput, calls=%fused_computation.6 | convolution fusion | flops 100663296 | bytes 1900544 | tf_op jit(solution)/shard_map/rk,ykn->yrn/dot_general | solution.py:180
  171.9 0.6 fusion.8
  172.5 0.6 gather_fusion.1
  173.2 8.4 %all_to_all.35 = bf16[4,64,192]{2,1,0:T(8,128)(2,1)S(1)} all-to-all(bf16[4,64,192]{2,1,0:T(8,128)(2,1)S(1)} %broadcast_select_fusion), channel_id=1, replica_groups=mesh['file'=2,'y'=4,'z'=8,'xl'=2,'core'=2] {'y'}, dimensions={0} | all-to-all | bytes 196608 | tf_op jit(solution)/shard_map/all_to_all | solution.py:130
  181.5 0.7 copy.28
  (31 shorter events, 0.2 us)
Async XLA Ops:
  1.9 10.7 %copy-start.2 = (bf16[128,4096]{1,0:T(8,128)(2,1)S(1)}, bf16[128,4096]{1,0:T(8,128)(2,1)}, u32[]{:S(2)}) copy-start(bf16[128,4096]{1,0:T(8,128)(2,1)} %param.6) | copy-start | bytes 3145732
  4.2 26.0 %all-to-all-start.1 = ((bf16[8,2,128,128]{3,2,1,0:T(8,128)(2,1)}), bf16[8,2,128,128]{3,2,1,0:T(8,128)(2,1)S(1)}, u32[]{:S(2)}, u32[]{:S(2)}) async-start(bf16[8,2,128,128]{3,2,1,0:T(8,128)(2,1)} %maximum_bitcast_fusion.1), calls=%async_computation.1 | async-start | bytes 1048576 | tf_op jit(solution)/shard_map/all_to_all | solution.py:130
  13.9 19.8 %copy-start.3 = (bf16[1024,192]{0,1:T(8,128)(2,1)S(1)}, bf16[1024,192]{0,1:T(8,128)(2,1)}, u32[]{:S(2)}) copy-start(bf16[1024,192]{0,1:T(8,128)(2,1)} %param.11) | copy-start | bytes 1179652
  30.2 39.8 %all-to-all-start.3 = ((bf16[8,128,256]{2,1,0:T(8,128)(2,1)}), bf16[8,128,256]{2,1,0:T(8,128)(2,1)S(1)}, u32[]{:S(2)}, u32[]{:S(2)}) async-start(bf16[8,128,256]{2,1,0:T(8,128)(2,1)} %get-tuple-element.15), calls=%async_computation.3 | async-start | bytes 1048576 | tf_op jit(solution)/shard_map/all_to_all | solution.py:130
  33.7 18.0 %collective-permute-start.6 = (bf16[1024,192]{0,1:T(8,128)(2,1)S(1)}, bf16[1024,192]{0,1:T(8,128)(2,1)}, u32[]{:S(2)}, u32[]{:S(2)}) collective-permute-start(bf16[1024,192]{0,1:T(8,128)(2,1)S(1)} %copy-done.3), channel_id=1, source_target_pairs={{0,96},{32,0},{64,32},{96,64},{1,97},{33,1},{65,33},{97,65},{2,98}... | collective-permute-start | bytes 1179656 | tf_op jit(solution)/shard_map/ppermute | solution.py:158
  36.8 16.9 %collective-permute-start.5 = (bf16[1024,192]{0,1:T(8,128)(2,1)S(1)}, bf16[1024,192]{0,1:T(8,128)(2,1)S(1)}, u32[]{:S(2)}, u32[]{:S(2)}) collective-permute-start(bf16[1024,192]{0,1:T(8,128)(2,1)S(1)} %copy-done.3), channel_id=1, source_target_pairs={{0,64},{32,96},{64,0},{96,32},{1,65},{33,97},{65,1},{97,33},{2,66}... | collective-permute-start | bytes 1179656 | tf_op jit(solution)/shard_map/ppermute | solution.py:158
  37.4 39.3 %collective-permute-start.4 = (bf16[1024,192]{0,1:T(8,128)(2,1)S(1)}, bf16[1024,192]{0,1:T(8,128)(2,1)}, u32[]{:S(2)}, u32[]{:S(2)}) collective-permute-start(bf16[1024,192]{0,1:T(8,128)(2,1)S(1)} %copy-done.3), channel_id=1, source_target_pairs={{0,32},{32,64},{64,96},{96,0},{1,33},{33,65},{65,97},{97,1},{2,34}... | collective-permute-start | bytes 1179656 | tf_op jit(solution)/shard_map/ppermute | solution.py:158
  38.4 41.6 %collective-permute-start = (bf16[8,2,128,128]{3,2,1,0:T(8,128)(2,1)S(1)}, bf16[8,2,128,128]{3,2,1,0:T(8,128)(2,1)S(1)}, u32[]{:S(2)}, u32[]{:S(2)}) collective-permute-start(bf16[8,2,128,128]{3,2,1,0:T(8,128)(2,1)S(1)} %all-to-all-done.1.refs_4_), channel_id=1, source_target_pairs={{0,1},{32,33},{64,65},{96,97},{1,2},{33,34},{65,66},{97,98},{2,3},... | collective-permute-start | bytes 1572872 | tf_op jit(solution)/shard_map/ppermute | solution.py:137
  40.3 39.7 %collective-permute-start.1 = (bf16[8,2,128,128]{3,2,1,0:T(8,128)(2,1)S(1)}, bf16[8,2,128,128]{3,2,1,0:T(8,128)(2,1)S(1)}, u32[]{:S(2)}, u32[]{:S(2)}) collective-permute-start(bf16[8,2,128,128]{3,2,1,0:T(8,128)(2,1)S(1)} %all-to-all-done.1.refs_4_), channel_id=1, source_target_pairs={{0,96},{32,1},{64,33},{96,65},{1,97},{33,2},{65,34},{97,66},{2,98}... | collective-permute-start | bytes 1572872 | tf_op jit(solution)/shard_map/ppermute | solution.py:137
  51.7 28.2 %collective-permute-start.2 = (bf16[8,2,128,128]{3,2,1,0:T(8,128)(2,1)S(1)}, bf16[8,2,128,128]{3,2,1,0:T(8,128)(2,1)S(1)}, u32[]{:S(2)}, u32[]{:S(2)}) collective-permute-start(bf16[8,2,128,128]{3,2,1,0:T(8,128)(2,1)S(1)} %all-to-all-done.1.refs_4_), channel_id=1, source_target_pairs={{0,64},{32,96},{64,1},{96,33},{1,65},{33,97},{65,2},{97,34},{2,66}... | collective-permute-start | bytes 1572872 | tf_op jit(solution)/shard_map/ppermute | solution.py:137
  53.6 0.8 copy-start.4
  54.4 26.0 %collective-permute-start.3 = (bf16[8,2,128,128]{3,2,1,0:T(8,128)(2,1)S(1)}, bf16[8,2,128,128]{3,2,1,0:T(8,128)(2,1)}, u32[]{:S(2)}, u32[]{:S(2)}) collective-permute-start(bf16[8,2,128,128]{3,2,1,0:T(8,128)(2,1)S(1)} %all-to-all-done.1.refs_4_), channel_id=1, source_target_pairs={{0,32},{32,64},{64,96},{96,1},{1,33},{33,65},{65,97},{97,2},{2,34}... | collective-permute-start | bytes 1572872 | tf_op jit(solution)/shard_map/ppermute | solution.py:137
  70.0 25.1 %all-to-all-start = ((bf16[8,128,256]{2,1,0:T(8,128)(2,1)}), bf16[8,128,256]{2,1,0:T(8,128)(2,1)S(1)}, u32[]{:S(2)}, u32[]{:S(2)}) async-start(bf16[8,128,256]{2,1,0:T(8,128)(2,1)} %get-tuple-element.14), calls=%async_computation | async-start | bytes 1048576 | tf_op jit(solution)/shard_map/all_to_all | solution.py:130
  79.9 43.9 %collective-permute-start.7 = (bf16[4,1024,192]{1,2,0:T(8,128)(2,1)}, bf16[4,1024,192]{1,2,0:T(8,128)(2,1)}, u32[]{:S(2)}, u32[]{:S(2)}) collective-permute-start(bf16[4,1024,192]{1,2,0:T(8,128)(2,1)} %get-tuple-element.13), channel_id=1, source_target_pairs={{0,2},{2,0},{1,3},{3,1},{4,6},{6,4},{5,7},{7,5},{8,10},{10,8},{9,1... | collective-permute-start | bytes 4718600 | tf_op jit(solution)/shard_map/ppermute | solution.py:162
  95.1 24.2 %all-to-all-start.4 = ((bf16[8,128,256]{2,1,0:T(8,128)(2,1)}), bf16[8,128,256]{2,1,0:T(8,128)(2,1)}, u32[]{:S(2)}, u32[]{:S(2)}) async-start(bf16[8,128,256]{2,1,0:T(8,128)(2,1)} %shard_map.78), calls=%async_computation.4 | async-start | bytes 1048576 | tf_op jit(solution)/shard_map/all_to_all | solution.py:130
  119.3 21.3 %all-to-all-start.2 = ((bf16[8,128,256]{2,1,0:T(8,128)(2,1)}), bf16[8,128,256]{2,1,0:T(8,128)(2,1)S(1)}, u32[]{:S(2)}, u32[]{:S(2)}) async-start(bf16[8,128,256]{2,1,0:T(8,128)(2,1)} %shard_map.77), calls=%async_computation.2 | async-start | bytes 1048576 | tf_op jit(solution)/shard_map/all_to_all | solution.py:130
  123.8 4.9 %copy-start.6 = (s32[8]{0:T(128)S(1)}, s32[8]{0:T(128)}, u32[]{:S(2)}) copy-start(s32[8]{0:T(128)} %param.9) | copy-start | bytes 100
  128.7 39.0 %collective-permute-start.8 = (bf16[2,4,1024,192]{2,3,1,0:T(8,128)(2,1)}, bf16[2,4,1024,192]{2,3,1,0:T(8,128)(2,1)}, u32[]{:S(2)}, u32[]{:S(2)}) collective-permute-start(bf16[2,4,1024,192]{2,3,1,0:T(8,128)(2,1)} %get-tuple-element.11), channel_id=1, source_target_pairs={{0,1},{1,0},{2,3},{3,2},{4,5},{5,4},{6,7},{7,6},{8,9},{9,8},{10,11... | collective-permute-start | bytes 9437192 | tf_op jit(solution)/shard_map/ppermute | solution.py:163
  142.4 1.4 copy-start.5
  142.9 21.6 %copy-start.1 = (bf16[128,4096]{1,0:T(8,128)(2,1)}, bf16[128,4096]{1,0:T(8,128)(2,1)S(1)}, u32[]{:S(2)}) copy-start(bf16[128,4096]{1,0:T(8,128)(2,1)S(1)} %copy.27) | copy-start | bytes 3145732
  144.7 19.4 %all-to-all-start.5 = ((bf16[8,8,4096]{2,1,0:T(8,128)(2,1)}), bf16[8,8,4096]{2,1,0:T(8,128)(2,1)S(1)}, u32[]{:S(2)}, u32[]{:S(2)}) async-start(bf16[8,8,4096]{2,1,0:T(8,128)(2,1)} %broadcast_in_dim.34), calls=%async_computation.5 | async-start | bytes 1048576 | tf_op jit(solution)/shard_map/all_to_all | solution.py:130
  167.7 4.2 %copy-start = (bf16[1,2,4,1024,192]{3,4,2,1,0:T(8,128)(2,1)S(1)}, bf16[1,2,4,1024,192]{3,4,2,1,0:T(8,128)(2,1)}, u32[]{:S(2)}) copy-start(bf16[1,2,4,1024,192]{3,4,2,1,0:T(8,128)(2,1)} %get-tuple-element.10) | copy-start | bytes 9437188

commit v2 on v1

v2 whole, which is shorter than its diff:
```python
import functools

import jax
import jax.numpy as jnp
from jax import lax
from jax.experimental import pallas as pl
from jax.experimental.pallas import tpu as pltpu
from jax.sharding import Mesh, PartitionSpec as P

D = 4096
HEADS = 32
KV_HEADS = 8
HEAD_DIM = 128
GROUP_HEADS = HEADS // KV_HEADS
GROUP_COLS = GROUP_HEADS * HEAD_DIM
ROWS = 128
MEM_ROWS = 8
STRIDE = ROWS // MEM_ROWS
EXTRA = 16
N_Z = 8
N_Y = 4
SPAN = ROWS * N_Z
SPAN_MEM = MEM_ROWS * N_Z
WINDOW = 4096
REACH = WINDOW + SPAN
PRIOR = WINDOW // SPAN
TILE = 256
CHUNK = 512
CALLS = 2
COEF = 1.4426950408889634 / HEAD_DIM**0.5
VMEM_LIMIT = 20 * 2**20
FIRST_LIMIT = 56 * 2**20
PLACES = ("y", "xl", "core")
GROUPS = 4 * N_Y
SWAP = [(0, 1), (1, 0)]


def scores_of(q, k):
    return lax.dot_general(q, k, (((1,), (1,)), ((), ())), preferred_element_type=jnp.float32)


def mix(p, v):
    return jnp.dot(p, v, preferred_element_type=jnp.float32)


def pack_kv_kernel(k_ref, v_ref, o_ref):
    for g in range(KV_HEADS):
        cols = slice(g * HEAD_DIM, (g + 1) * HEAD_DIM)
        o_ref[g, 0] = k_ref[:, cols]
        o_ref[g, 1] = v_ref[:, cols]


def pack_kv(keys, values):
    return pl.pallas_call(
        pack_kv_kernel,
        out_shape=jax.ShapeDtypeStruct((KV_HEADS, 2, ROWS, HEAD_DIM), keys.dtype),
        compiler_params=pltpu.CompilerParams(vmem_limit_bytes=VMEM_LIMIT),
        cost_estimate=pl.CostEstimate(flops=0, bytes_accessed=2**20, transcendentals=0),
    )(keys, values)


def pack_q_kernel(pos_ref, q_ref, o_ref):
    row = lax.broadcasted_iota(jnp.int32, (EXTRA, ROWS), 0)
    col = lax.broadcasted_iota(jnp.int32, (EXTRA, ROWS), 1)
    pick = jnp.zeros((EXTRA, ROWS), jnp.float32)
    offset = jnp.zeros((EXTRA, 1), jnp.int32)
    for j in range(MEM_ROWS):
        pos = pos_ref[j]
        pick = jnp.where((row == j) & (col == pos % ROWS), 1.0, pick)
        offset = jnp.where(row[:, :1] == MEM_ROWS + j, pos % STRIDE, offset)
    pick = pick.astype(jnp.bfloat16)
    offset = offset.astype(jnp.float32)
    for g in range(N_Z):
        q = q_ref[:, g * GROUP_COLS : (g + 1) * GROUP_COLS]
        o_ref[g, :ROWS] = q
        o_ref[g, ROWS:] = (mix(pick, q) + offset).astype(jnp.bfloat16)


def pack_q(mem_pos, queries):
    return pl.pallas_call(
        pack_q_kernel,
        in_specs=[
            pl.BlockSpec(memory_space=pltpu.SMEM),
            pl.BlockSpec(memory_space=pltpu.VMEM),
        ],
        out_shape=jax.ShapeDtypeStruct((N_Z, ROWS + EXTRA, GROUP_COLS), queries.dtype),
        compiler_params=pltpu.CompilerParams(vmem_limit_bytes=VMEM_LIMIT),
        cost_estimate=pl.CostEstimate(flops=2**27, bytes_accessed=2**21, transcendentals=0),
    )(mem_pos, queries)


def first_kernel(absent_ref, q_ref, *refs):
    pieces, (k_all, v_all, o_ref) = refs[: PRIOR + 1], refs[PRIOR + 1 :]
    for slot, piece in enumerate(pieces):
        for z in range(N_Z):
            at = pl.ds(slot * SPAN + z * ROWS, ROWS)
            k_all[at, :] = piece[z, 0]
            v_all[at, :HEAD_DIM] = piece[z, 1]
            v_all[at, HEAD_DIM:] = jnp.ones((ROWS, HEAD_DIM), jnp.bfloat16)
    absent = absent_ref[0]
    for slot in range(PRIOR):

        @pl.when(slot < absent)
        def _():
            first = k_all[pl.ds(pl.multiple_of(absent * SPAN, SPAN), 16), :][:1, :]
            at = pl.ds(slot * SPAN, SPAN)
            k_all[at, :] = jnp.broadcast_to(first, (SPAN, HEAD_DIM))
            v_all[at, :] = jnp.zeros((SPAN, 2 * HEAD_DIM), jnp.bfloat16)

    extra = [q_ref[z, ROWS:].astype(jnp.float32) for z in range(N_Z)]
    q = jnp.concatenate(
        [
            extra[z][:MEM_ROWS, h * HEAD_DIM : (h + 1) * HEAD_DIM]
            for h in range(GROUP_HEADS)
            for z in range(N_Z)
        ]
    ).astype(jnp.bfloat16)
    offset = jnp.concatenate([extra[z][MEM_ROWS:, :HEAD_DIM] for z in range(N_Z)])[:, :1]
    place = STRIDE * lax.broadcasted_iota(jnp.int32, (SPAN_MEM, 1), 0) + offset.astype(jnp.int32)
    place = jnp.concatenate([place] * GROUP_HEADS)
    count = GROUP_HEADS * SPAN_MEM
    peak = jnp.full((count, 1), -jnp.inf, jnp.float32)
    total = jnp.zeros((count, 2 * HEAD_DIM), jnp.float32)
    for start in (*range(WINDOW, REACH, CHUNK), *range(0, WINDOW, CHUNK)):
        s = scores_of(q, k_all[start : start + CHUNK, :])
        key = start + lax.broadcasted_iota(jnp.int32, (1, CHUNK), 1)
        if start >= WINDOW:
            s = jnp.where(key - WINDOW <= place, s, -jnp.inf)
        if start < SPAN:
            s = jnp.where(key > place, s, -jnp.inf)
        higher = jnp.maximum(peak, jnp.max(s, axis=1, keepdims=True))
        fade = jnp.exp2(peak * COEF - higher * COEF)
        p = jnp.exp2(s * COEF - higher * COEF).astype(jnp.bfloat16)
        total = total * fade + mix(p, v_all[start : start + CHUNK, :])
        peak = higher
    out = (total[:, :HEAD_DIM] / total[:, HEAD_DIM:]).astype(jnp.bfloat16)
    for z in range(N_Z):
        for h in range(GROUP_HEADS):
            o_ref[z, :, h * HEAD_DIM : (h + 1) * HEAD_DIM] = out[
                h * SPAN_MEM : (h + 1) * SPAN_MEM, :
            ]


def attend_first(q, pieces, absent):
    return pl.pallas_call(
        first_kernel,
        in_specs=[pl.BlockSpec(memory_space=pltpu.SMEM)]
        + [pl.BlockSpec(memory_space=pltpu.VMEM)] * (PRIOR + 2),
        out_shape=(
            jax.ShapeDtypeStruct((REACH, HEAD_DIM), q.dtype),
            jax.ShapeDtypeStruct((REACH, 2 * HEAD_DIM), q.dtype),
            jax.ShapeDtypeStruct((N_Z, SPAN_MEM, GROUP_COLS), q.dtype),
        ),
        compiler_params=pltpu.CompilerParams(vmem_limit_bytes=FIRST_LIMIT),
        cost_estimate=pl.CostEstimate(
            flops=GROUP_HEADS * SPAN_MEM * REACH * HEAD_DIM * 8,
            bytes_accessed=8 * 2**20,
            transcendentals=GROUP_HEADS * SPAN_MEM * REACH,
        ),
    )(absent, q, *pieces)


def attend_kernel(heads, q_ref, k_all, v_all, o_ref, q_rows):
    step = pl.program_id(0)
    blocks = TILE // ROWS
    count = heads * TILE
    for h in range(heads):
        for b in range(blocks):
            q_rows[h * TILE + b * ROWS : h * TILE + (b + 1) * ROWS, :] = q_ref[
                b, :ROWS, h * HEAD_DIM : (h + 1) * HEAD_DIM
            ]
    q = q_rows[...]
    start = step * TILE

    def window(ref, offset, size):
        return ref[pl.ds(pl.multiple_of(start + offset, TILE), size), :]

    row = lax.broadcasted_iota(jnp.int32, (1, TILE, TILE), 1)
    col = lax.broadcasted_iota(jnp.int32, (1, TILE, TILE), 2)
    own = col <= row
    oldest = scores_of(q, window(k_all, 0, TILE)).reshape(heads, TILE, TILE)
    newest = scores_of(q, window(k_all, WINDOW, TILE)).reshape(heads, TILE, TILE)
    s = jnp.where(own, newest, oldest).reshape(count, TILE)
    peak = jnp.max(s, axis=1, keepdims=True)
    p = jnp.exp2(s * COEF - peak * COEF).astype(jnp.bfloat16).reshape(heads, TILE, TILE)
    zero = jnp.zeros((), jnp.bfloat16)
    total = mix(jnp.where(own, p, zero).reshape(count, TILE), window(v_all, WINDOW, TILE))
    total += mix(jnp.where(own, zero, p).reshape(count, TILE), window(v_all, 0, TILE))
    offset = TILE
    while offset < WINDOW:
        size = min(CHUNK, WINDOW - offset)
        s = scores_of(q, window(k_all, offset, size))
        higher = jnp.maximum(peak, jnp.max(s, axis=1, keepdims=True))
        fade = jnp.exp2(peak * COEF - higher * COEF)
        p = jnp.exp2(s * COEF - higher * COEF).astype(jnp.bfloat16)
        total = total * fade + mix(p, window(v_all, offset, size))
        peak = higher
        offset += size
    out = (total[:, :HEAD_DIM] / total[:, HEAD_DIM:]).astype(jnp.bfloat16)
    for h in range(heads):
        for b in range(blocks):
            o_ref[b, :, h * HEAD_DIM : (h + 1) * HEAD_DIM] = out[
                h * TILE + b * ROWS : h * TILE + (b + 1) * ROWS, :
            ]


def attend(q, k_all, v_all, part):
    heads = GROUP_HEADS // CALLS
    cols = heads * HEAD_DIM
    blocks = TILE // ROWS
    return pl.pallas_call(
        functools.partial(attend_kernel, heads),
        grid=(SPAN // TILE,),
        in_specs=[
            pl.BlockSpec((blocks, ROWS + EXTRA, cols), lambda i: (i, 0, part)),
            pl.BlockSpec((REACH, HEAD_DIM), lambda i: (0, 0)),
            pl.BlockSpec((REACH, 2 * HEAD_DIM), lambda i: (0, 0)),
        ],
        out_specs=pl.BlockSpec((blocks, ROWS, cols), lambda i: (i, 0, 0)),
        scratch_shapes=[pltpu.VMEM((heads * TILE, HEAD_DIM), jnp.bfloat16)],
        out_shape=jax.ShapeDtypeStruct((N_Z, ROWS, cols), q.dtype),
        compiler_params=pltpu.CompilerParams(vmem_limit_bytes=VMEM_LIMIT),
        cost_estimate=pl.CostEstimate(
            flops=heads * SPAN * WINDOW * HEAD_DIM * 8,
            bytes_accessed=4 * 2**20,
            transcendentals=heads * SPAN * WINDOW,
        ),
    )(q, k_all, v_all)


def unpack_kernel(*refs):
    parts, o_ref = refs[:-1], refs[-1]
    cols = GROUP_COLS // len(parts)
    for g in range(N_Z):
        for c, part in enumerate(parts):
            at = g * GROUP_COLS + c * cols
            o_ref[:, at : at + cols] = part[g]


def unpack(parts):
    return pl.pallas_call(
        unpack_kernel,
        out_shape=jax.ShapeDtypeStruct((ROWS, D), parts[0].dtype),
        compiler_params=pltpu.CompilerParams(vmem_limit_bytes=VMEM_LIMIT),
        cost_estimate=pl.CostEstimate(flops=0, bytes_accessed=2**21, transcendentals=0),
    )(*parts)


def summary_kernel(place_ref, *refs):
    rows, gain_ref, weights = refs[:N_Y], refs[N_Y], refs[N_Y + 1 : N_Y + 5]
    o_ref, normed = refs[N_Y + 5 :]
    y, xl, core = place_ref[0], place_ref[1], place_ref[2]
    for back, rows_ref in enumerate(rows):
        squares = jnp.zeros((SPAN_MEM, 1), jnp.float32)
        for z in range(N_Z):
            picked = rows_ref[z].astype(jnp.float32)
            squares += jnp.sum(picked * picked, axis=1, keepdims=True)
        factor = lax.rsqrt(squares / D + 1e-05)
        at = pl.ds(pl.multiple_of((y - back + N_Y) % N_Y * SPAN_MEM, SPAN_MEM), SPAN_MEM)
        for z in range(N_Z):
            gain = gain_ref[:, z * GROUP_COLS : (z + 1) * GROUP_COLS]
            picked = rows_ref[z].astype(jnp.float32)
            normed[z, at, :] = (picked * factor * gain).astype(jnp.bfloat16)
    total = jnp.zeros(o_ref.shape, jnp.float32)
    half = N_Z // 4
    for i, w_ref in enumerate(weights):
        tp = (xl + i // 2) % 2 * 2 + (core + i % 2) % 2
        for k in range(half):
            cols = slice(k * GROUP_COLS, (k + 1) * GROUP_COLS)
            total += scores_of(w_ref[:, cols], normed[tp * half + k])
    o_ref[...] = total.astype(jnp.bfloat16)


def summarize(place, rows, gain, weights):
    cols = weights[0].shape[0]
    vmem = pl.BlockSpec(memory_space=pltpu.VMEM)
    return pl.pallas_call(
        summary_kernel,
        in_specs=[pl.BlockSpec(memory_space=pltpu.SMEM)] + [vmem] * (N_Y + 5),
        scratch_shapes=[pltpu.VMEM((N_Z, N_Y * SPAN_MEM, GROUP_COLS), jnp.bfloat16)],
        out_shape=jax.ShapeDtypeStruct((cols, N_Y * SPAN_MEM), jnp.bfloat16),
        compiler_params=pltpu.CompilerParams(vmem_limit_bytes=VMEM_LIMIT),
        cost_estimate=pl.CostEstimate(
            flops=2 * N_Y * SPAN_MEM * D * cols,
            bytes_accessed=4 * 2**20,
            transcendentals=0,
        ),
    )(place, *rows, gain.reshape(1, D), *weights)


def together(*values):
    return lax.optimization_barrier(values)


def exchange(a, axis):
    return lax.all_to_all(a, axis, split_axis=0, concat_axis=0, tiled=True)


def from_group_behind(a, back):
    def index(group):
        return group % N_Y * (GROUPS // N_Y) + group // N_Y

    return lax.ppermute(a, PLACES, [(index(g - back), index(g)) for g in range(back, GROUPS)])


def on_device(queries, keys, values, mem_pos, norm_gain, summary_weight):
    xl, core, y = lax.axis_index("xl"), lax.axis_index("core"), lax.axis_index("y")
    place = (xl * 2 + core) * N_Y + y
    absent = jnp.maximum(PRIOR - place, 0).astype(jnp.int32).reshape(1)

    kv = pack_kv(keys, values)
    own = exchange(kv, "z")
    weight, _ = together(summary_weight.T, kv)
    across = lax.ppermute(weight, "xl", SWAP)
    beside = lax.ppermute(weight, "core", SWAP)
    weights = [weight, beside, across, lax.ppermute(across, "core", SWAP)]
    own, q, weights = together(own, pack_q(mem_pos, queries), weights)
    q = exchange(q, "z")
    pieces = [from_group_behind(own, back) for back in range(PRIOR, 0, -1)] + [own]
    k_all, v_all, picked = attend_first(q, pieces, absent)

    picked = exchange(picked, "z")
    out, picked = together(attend(q, k_all, v_all, 0), picked)
    rows = [picked] + [
        lax.ppermute(picked, "y", [(i, (i + back) % N_Y) for i in range(N_Y)])
        for back in range(1, N_Y)
    ]
    sent = [exchange(out, "z")]
    for part in range(1, CALLS):
        out, sent = together(attend(q, k_all, v_all, part), sent)
        if part == CALLS - 1:
            out, rows[1], rows[3] = together(out, rows[1], rows[3])
        sent = sent + [exchange(out, "z")]
    summary = summarize(jnp.stack((y, xl, core)), rows, norm_gain, weights)
    sent, summary = together(sent, summary)
    return unpack(sent), summary.T


def solution(mesh):
    split = Mesh(mesh.devices.reshape(-1, N_Y, N_Z, 2, 2), ("file", "y", "z", "xl", "core"))
    tokens = ("file", "xl", "core", "y", "z")
    return jax.shard_map(
        on_device,
        mesh=split,
        in_specs=(
            P(tokens, None),
            P(tokens, None),
            P(tokens, None),
            P(tokens),
            P(),
            P(("xl", "core"), ("y", "z")),
        ),
        out_specs=(P(tokens, None), P(("file", "xl", "core"), ("y", "z"))),
        check_vma=False,
    )
```

time: 183 us -> 151 us (0.83)
  the two profiles are of different devices: /device:TPU:2 before, /device:TPU:4 now
where the time goes in v2:
time: 151 us
  starting transfers between devices  53.6 us (35%)
  waiting for transfers between devices  42 us (28%)
  Pallas kernels  39 us (26%)
  local copies, waits for them, and re-layouts  15.1 us (10%)
    all_to_all x5, starting transfers between devices, exchange(): return lax.all_to_all(a, axis, split_axis=0, concat_axis=0, tiled=True)  32.2 us
    pallas_call x2, Pallas kernels, attend(): pl.pallas_call(functools.partial(attend_kernel, heads), grid=(SPAN // TIL...  26.5 us
    ppermute x4, waiting for transfers between devices, from_group_behind(): lax.ppermute(a, PLACES, [(index(g - back), index(g)) for g in range(back,...  15.9 us
    unnamed x48, local copies, waits for them, and re-layouts  15.1 us
    ppermute x4, starting transfers between devices, from_group_behind(): lax.ppermute(a, PLACES, [(index(g - back), index(g)) for g in range(back,...  14.7 us
    ppermute x3, waiting for transfers between devices, on_device(): lax.ppermute(picked, 'y', [(i, (i + back) % N_Y) for i in range(N_Y)])  11.9 us
    ppermute x1, waiting for transfers between devices, on_device(): across = lax.ppermute(weight, 'xl', SWAP)  9.37 us
    pallas_call x1, Pallas kernels, attend_first(): pl.pallas_call(first_kernel, in_specs=[pl.BlockSpec(memory_space=pltpu.SM...  5.72 us
  transfers between devices with their start and end apart: 15, of which 7 were waited for; matrix products, arithmetic and copies ran while one was open for 0% of the time, Pallas kernels for 21%

profile of v2, /device:TPU:4, one launch (start us, length us, event | category | flops | bytes accessed | tf_op | source)
XLA Modules:
  0.0 150.5 jit_solution(11858114072039982310)
XLA Ops:
  0.6 0.0 copy-start.4
  0.7 1.0 copy-done.12
  1.7 0.9 copy-done.13
  2.7 0.9 shard_map.77
  3.6 8.5 %all-to-all-start = ((bf16[8,2,128,128]{3,2,1,0:T(8,128)(2,1)}), bf16[8,2,128,128]{3,2,1,0:T(8,128)(2,1)S(1)}, u32[]{:S(2)}, u32[]{:S(2)}) async-start(bf16[8,2,128,128]{3,2,1,0:T(8,128)(2,1)} %shard_map.77), calls=%async_computation | async-start | bytes 1048576 | tf_op jit(solution)/shard_map/all_to_all | solution.py:296
  12.0 1.3 collective-permute-start.1
  13.3 0.0 collective-permute-start
  13.3 9.4 %collective-permute-done.1.refs_7_ = bf16[192,1024]{1,0:T(8,128)(2,1)S(1)} collective-permute-done((bf16[192,1024]{1,0:T(8,128)(2,1)S(1)}, bf16[192,1024]{1,0:T(8,128)(2,1)S(1)}, u32[]{:S(2)}, u32[]{:S(2)}) %collective-permute-start.1) | collective-permute-done | bytes 393248 | tf_op jit(solution)/shard_map/ppermute | solution.py:314
  22.7 0.0 collective-permute-start.2
  22.7 1.9 %shard_map.78 = bf16[8,144,512]{2,1,0:T(8,128)(2,1)} custom-call(s32[8]{0:T(128)S(1)} %copy-done.15, bf16[128,4096]{1,0:T(8,128)(2,1)S(1)} %copy-done.3), custom_call_target="tpu_custom_call" | custom-call | flops 134217728 | bytes 2097152 | tf_op jit(solution)/shard_map/pallas_call | solution.py:80
  24.6 0.8 copy-done.8
  25.4 0.8 copy-done.10
  26.2 3.3 %all-to-all-done.refs_4_ = bf16[8,2,128,128]{3,2,1,0:T(8,128)(2,1)S(1)} async-done(((bf16[8,2,128,128]{3,2,1,0:T(8,128)(2,1)}), bf16[8,2,128,128]{3,2,1,0:T(8,128)(2,1)S(1)}, u32[]{:S(2)}, u32[]{:S(2)}) %all-to-all-start) | async-done | bytes 524320 | tf_op jit(solution)/shard_map/all_to_all | solution.py:296
  29.5 3.6 %all-to-all-start.1 = ((bf16[8,144,512]{2,1,0:T(8,128)(2,1)}), bf16[8,144,512]{2,1,0:T(8,128)(2,1)S(1)}, u32[]{:S(2)}, u32[]{:S(2)}) async-start(bf16[8,144,512]{2,1,0:T(8,128)(2,1)} %shard_map.78), calls=%async_computation.1 | async-start | bytes 2359296 | tf_op jit(solution)/shard_map/all_to_all | solution.py:296
  33.1 3.5 %collective-permute-start.6 = (bf16[8,2,128,128]{3,2,1,0:T(8,128)(2,1)S(1)}, bf16[8,2,128,128]{3,2,1,0:T(8,128)(2,1)S(1)}, u32[]{:S(2)}, u32[]{:S(2)}) collective-permute-start(bf16[8,2,128,128]{3,2,1,0:T(8,128)(2,1)S(1)} %all-to-all-done.refs_4_), channel_id=1, source_target_pairs={{0,32},{32,64},{64,96},{96,1},{1,33},{33,65},{65,97},{97,2},{2,34}... | collective-permute-start | bytes 1572872 | tf_op jit(solution)/shard_map/ppermute | solution.py:303
  36.6 4.8 %collective-permute-start.5 = (bf16[8,2,128,128]{3,2,1,0:T(8,128)(2,1)S(1)}, bf16[8,2,128,128]{3,2,1,0:T(8,128)(2,1)S(1)}, u32[]{:S(2)}, u32[]{:S(2)}) collective-permute-start(bf16[8,2,128,128]{3,2,1,0:T(8,128)(2,1)S(1)} %all-to-all-done.refs_4_), channel_id=1, source_target_pairs={{0,64},{32,96},{64,1},{96,33},{1,65},{33,97},{65,2},{97,34},{2,66}... | collective-permute-start | bytes 1572872 | tf_op jit(solution)/shard_map/ppermute | solution.py:303
  41.4 2.7 %collective-permute-start.4 = (bf16[8,2,128,128]{3,2,1,0:T(8,128)(2,1)S(1)}, bf16[8,2,128,128]{3,2,1,0:T(8,128)(2,1)S(1)}, u32[]{:S(2)}, u32[]{:S(2)}) collective-permute-start(bf16[8,2,128,128]{3,2,1,0:T(8,128)(2,1)S(1)} %all-to-all-done.refs_4_), channel_id=1, source_target_pairs={{0,96},{32,1},{64,33},{96,65},{1,97},{33,2},{65,34},{97,66},{2,98}... | collective-permute-start | bytes 1572872 | tf_op jit(solution)/shard_map/ppermute | solution.py:303
  44.2 3.7 %collective-permute-start.3 = (bf16[8,2,128,128]{3,2,1,0:T(8,128)(2,1)S(1)}, bf16[8,2,128,128]{3,2,1,0:T(8,128)(2,1)}, u32[]{:S(2)}, u32[]{:S(2)}) collective-permute-start(bf16[8,2,128,128]{3,2,1,0:T(8,128)(2,1)S(1)} %all-to-all-done.refs_4_), channel_id=1, source_target_pairs={{0,1},{32,33},{64,65},{96,97},{1,2},{33,34},{65,66},{97,98},{2,3},... | collective-permute-start | bytes 1572872 | tf_op jit(solution)/shard_map/ppermute | solution.py:303
  47.8 1.0 collective-permute-done.6.refs_3_
  48.8 10.5 %collective-permute-done.5.refs_2_ = bf16[8,2,128,128]{3,2,1,0:T(8,128)(2,1)S(1)} collective-permute-done((bf16[8,2,128,128]{3,2,1,0:T(8,128)(2,1)S(1)}, bf16[8,2,128,128]{3,2,1,0:T(8,128)(2,1)S(1)}, u32[]{:S(2)}, u32[]{:S(2)}) %collective-permute-start.5) | collective-permute-done | bytes 524320 | tf_op jit(solution)/shard_map/ppermute | solution.py:303
  59.3 4.4 %collective-permute-done.4.refs_1_ = bf16[8,2,128,128]{3,2,1,0:T(8,128)(2,1)S(1)} collective-permute-done((bf16[8,2,128,128]{3,2,1,0:T(8,128)(2,1)S(1)}, bf16[8,2,128,128]{3,2,1,0:T(8,128)(2,1)S(1)}, u32[]{:S(2)}, u32[]{:S(2)}) %collective-permute-start.4) | collective-permute-done | bytes 524320 | tf_op jit(solution)/shard_map/ppermute | solution.py:303
  63.7 0.0 collective-permute-done.3.refs_0_
  63.7 1.5 %all-to-all-done.1.q_ref = bf16[8,144,512]{2,1,0:T(8,128)(2,1)S(1)} async-done(((bf16[8,144,512]{2,1,0:T(8,128)(2,1)}), bf16[8,144,512]{2,1,0:T(8,128)(2,1)S(1)}, u32[]{:S(2)}, u32[]{:S(2)}) %all-to-all-start.1) | async-done | bytes 1179680 | tf_op jit(solution)/shard_map/all_to_all | solution.py:296
  65.3 1.0 copy-done
  66.4 5.7 %shard_map.79 = (bf16[5120,128]{1,0:T(8,128)(2,1)}, bf16[5120,256]{1,0:T(8,128)(2,1)}, bf16[8,64,512]{2,1,0:T(8,128)(2,1)}) custom-call(s32[1]{0:T(128)} %bitcast.1.absent_ref, bf16[8,144,512]{2,1,0:T(8,128)(2,1)} %copy-done, bf16[8,2,128,128]{3,2,1,0:T(8,128)(2,1)} %collective-permute-done.3.refs_0_, bf16[8,2,128,128]{3,2,1,0:T(8,128)(2,1)} %copy-done.23, ...), custom_call_target="tpu_custom_call" | custom-call | flops 1342177280 | bytes 8388608 | tf_op jit(solution)/shard_map/pallas_call | solution.py:145
  72.1 5.7 %all-to-all-start.2 = ((bf16[8,64,512]{2,1,0:T(8,128)(2,1)}), bf16[8,64,512]{2,1,0:T(8,128)(2,1)S(1)}, u32[]{:S(2)}, u32[]{:S(2)}) async-start(bf16[8,64,512]{2,1,0:T(8,128)(2,1)} %get-tuple-element.27), calls=%async_computation.2 | async-start | bytes 1048576 | tf_op jit(solution)/shard_map/all_to_all | solution.py:296
  77.8 1.3 copy-done.1
  79.1 1.7 %copy-done.16 = bf16[5120,256]{1,0:T(8,128)(2,1)S(1)} copy-done((bf16[5120,256]{1,0:T(8,128)(2,1)S(1)}, bf16[5120,256]{1,0:T(8,128)(2,1)}, u32[]{:S(2)}) %copy-start.16) | copy-done | bytes 2621464
  80.8 1.3 copy-done.18
  82.2 13.3 %shard_map.81 = bf16[8,128,256]{2,1,0:T(8,128)(2,1)} custom-call(bf16[8,144,512]{2,1,0:T(8,128)(2,1)S(1)} %copy-done.1, bf16[5120,128]{1,0:T(8,128)(2,1)S(1)} %copy-done.18, bf16[5120,256]{1,0:T(8,128)(2,1)S(1)} %copy-done.16), custom_call_target="tpu_custom_call" | custom-call | flops 8589934592 | bytes 4194304 | tf_op jit(solution)/shard_map/pallas_call | solution.py:211
  95.4 0.0 all-to-all-done.2.refs_0_
  95.4 7.2 %all-to-all-start.3 = ((bf16[8,128,256]{2,1,0:T(8,128)(2,1)}), bf16[8,128,256]{2,1,0:T(8,128)(2,1)S(1)}, u32[]{:S(2)}, u32[]{:S(2)}) async-start(bf16[8,128,256]{2,1,0:T(8,128)(2,1)} %shard_map.81), calls=%async_computation.3 | async-start | bytes 1048576 | tf_op jit(solution)/shard_map/all_to_all | solution.py:296
  102.6 3.6 %collective-permute-start.8 = (bf16[8,64,512]{2,1,0:T(8,128)(2,1)S(1)}, bf16[8,64,512]{2,1,0:T(8,128)(2,1)S(1)}, u32[]{:S(2)}, u32[]{:S(2)}) collective-permute-start(bf16[8,64,512]{2,1,0:T(8,128)(2,1)S(1)} %all-to-all-done.2.refs_0_), channel_id=1, source_target_pairs={{0,96},{32,0},{64,32},{96,64},{1,97},{33,1},{65,33},{97,65},{2,98}... | collective-permute-start | bytes 1572872 | tf_op jit(solution)/shard_map/ppermute | solution.py:325
  106.2 0.0 collective-permute-start.7
  106.2 1.7 %copy-done.17 = bf16[5120,256]{1,0:T(8,128)(2,1)S(1)} copy-done((bf16[5120,256]{1,0:T(8,128)(2,1)S(1)}, bf16[5120,256]{1,0:T(8,128)(2,1)}, u32[]{:S(2)}) %copy-start.17) | copy-done | bytes 2621464
  108.0 1.3 copy-done.19
  109.3 13.3 %shard_map.80 = bf16[8,128,256]{2,1,0:T(8,128)(2,1)} custom-call(bf16[8,144,512]{2,1,0:T(8,128)(2,1)S(1)} %copy-done.2, bf16[5120,128]{1,0:T(8,128)(2,1)S(1)} %copy-done.19, bf16[5120,256]{1,0:T(8,128)(2,1)S(1)} %copy-done.17), custom_call_target="tpu_custom_call" | custom-call | flops 8589934592 | bytes 4194304 | tf_op jit(solution)/shard_map/pallas_call | solution.py:211
  122.6 0.0 collective-permute-done.7.refs_1_
  122.6 7.3 %all-to-all-start.4 = ((bf16[8,128,256]{2,1,0:T(8,128)(2,1)}), bf16[8,128,256]{2,1,0:T(8,128)(2,1)S(1)}, u32[]{:S(2)}, u32[]{:S(2)}) async-start(bf16[8,128,256]{2,1,0:T(8,128)(2,1)} %shard_map.80), calls=%async_computation.4 | async-start | bytes 1048576 | tf_op jit(solution)/shard_map/all_to_all | solution.py:296
  129.8 1.7 %collective-permute-start.9 = (bf16[8,64,512]{2,1,0:T(8,128)(2,1)S(1)}, bf16[8,64,512]{2,1,0:T(8,128)(2,1)S(1)}, u32[]{:S(2)}, u32[]{:S(2)}) collective-permute-start(bf16[8,64,512]{2,1,0:T(8,128)(2,1)S(1)} %all-to-all-done.2.refs_0_), channel_id=1, source_target_pairs={{0,64},{32,96},{64,0},{96,32},{1,65},{33,97},{65,1},{97,33},{2,66}... | collective-permute-start | bytes 1572872 | tf_op jit(solution)/shard_map/ppermute | solution.py:325
  131.6 0.1 pad_add_fusion.place_ref
  131.7 11.9 %collective-permute-done.9.refs_2_ = bf16[8,64,512]{2,1,0:T(8,128)(2,1)S(1)} collective-permute-done((bf16[8,64,512]{2,1,0:T(8,128)(2,1)S(1)}, bf16[8,64,512]{2,1,0:T(8,128)(2,1)S(1)}, u32[]{:S(2)}, u32[]{:S(2)}) %collective-permute-start.9) | collective-permute-done | bytes 524320 | tf_op jit(solution)/shard_map/ppermute | solution.py:325
  143.6 1.0 copy-done.7
  144.6 1.0 copy-done.9
  145.6 1.0 copy-done.11
  146.5 2.9 %shard_map.82 = bf16[192,256]{1,0:T(8,128)(2,1)} custom-call(s32[3]{0:T(128)S(1)} %pad_add_fusion.place_ref, bf16[8,64,512]{2,1,0:T(8,128)(2,1)S(1)} %all-to-all-done.2.refs_0_, bf16[8,64,512]{2,1,0:T(8,128)(2,1)S(1)} %collective-permute-done.7.refs_1_, bf16[8,64,512]{2,1,0:T(8,128)(2,1)S(1)} %collective-permute-done.9.refs_2_, ...), custom_call_target="tpu_custom_call" | custom-call | flops 402653184 | bytes 4194304 | tf_op jit(solution)/shard_map/pallas_call | solution.py:277
  149.5 0.0 all-to-all-done.4.refs_1_
  149.5 1.1 shard_map.83
  (38 shorter events, 0.1 us)
Async XLA Ops:
  0.6 11.4 %copy-start.4 = (bf16[1024,192]{0,1:T(8,128)(2,1)S(1)}, bf16[1024,192]{0,1:T(8,128)(2,1)}, u32[]{:S(2)}) copy-start(bf16[1024,192]{0,1:T(8,128)(2,1)} %param.11) | copy-start | bytes 1179652
  0.6 22.0 %copy-start.3 = (bf16[128,4096]{1,0:T(8,128)(2,1)S(1)}, bf16[128,4096]{1,0:T(8,128)(2,1)}, u32[]{:S(2)}) copy-start(bf16[128,4096]{1,0:T(8,128)(2,1)} %q_ref.1) | copy-start | bytes 3145732
  0.7 1.1 copy-start.12
  1.7 0.9 copy-start.13
  2.7 20.0 %copy-start.15 = (s32[8]{0:T(128)S(1)}, s32[8]{0:T(128)}, u32[]{:S(2)}) copy-start(s32[8]{0:T(128)} %pos_ref.1) | copy-start | bytes 100
  3.6 26.0 %all-to-all-start = ((bf16[8,2,128,128]{3,2,1,0:T(8,128)(2,1)}), bf16[8,2,128,128]{3,2,1,0:T(8,128)(2,1)S(1)}, u32[]{:S(2)}, u32[]{:S(2)}) async-start(bf16[8,2,128,128]{3,2,1,0:T(8,128)(2,1)} %shard_map.77), calls=%async_computation | async-start | bytes 1048576 | tf_op jit(solution)/shard_map/all_to_all | solution.py:296
  12.0 10.7 %collective-permute-start.1 = (bf16[192,1024]{1,0:T(8,128)(2,1)S(1)}, bf16[192,1024]{1,0:T(8,128)(2,1)S(1)}, u32[]{:S(2)}, u32[]{:S(2)}) collective-permute-start(bf16[192,1024]{1,0:T(8,128)(2,1)S(1)} %bitcast.7), channel_id=1, source_target_pairs={{0,2},{2,0},{1,3},{3,1},{4,6},{6,4},{5,7},{7,5},{8,10},{10,8},{9,1... | collective-permute-start | bytes 1179656 | tf_op jit(solution)/shard_map/ppermute | solution.py:314
  13.3 11.3 %collective-permute-start = (bf16[192,1024]{1,0:T(8,128)(2,1)S(1)}, bf16[192,1024]{1,0:T(8,128)(2,1)S(1)}, u32[]{:S(2)}, u32[]{:S(2)}) collective-permute-start(bf16[192,1024]{1,0:T(8,128)(2,1)S(1)} %bitcast.8), channel_id=1, source_target_pairs={{0,1},{1,0},{2,3},{3,2},{4,5},{5,4},{6,7},{7,6},{8,9},{9,8},{10,11... | collective-permute-start | bytes 1179656 | tf_op jit(solution)/shard_map/ppermute | solution.py:315
  22.7 1.9 %copy-start.6 = (bf16[192,1024]{1,0:T(8,128)(2,1)}, bf16[192,1024]{1,0:T(8,128)(2,1)S(1)}, u32[]{:S(2)}) copy-start(bf16[192,1024]{1,0:T(8,128)(2,1)S(1)} %collective-permute-done.1.refs_7_) | copy-start | bytes 1179652
  22.7 2.7 %collective-permute-start.2 = (bf16[192,1024]{1,0:T(8,128)(2,1)S(1)}, bf16[192,1024]{1,0:T(8,128)(2,1)S(1)}, u32[]{:S(2)}, u32[]{:S(2)}) collective-permute-start(bf16[192,1024]{1,0:T(8,128)(2,1)S(1)} %collective-permute-done.1.refs_7_), channel_id=1, source_target_pairs={{0,1},{1,0},{2,3},{3,2},{4,5},{5,4},{6,7},{7,6},{8,9},{9,8},{10,11... | collective-permute-start | bytes 1179656 | tf_op jit(solution)/shard_map/ppermute | solution.py:316
  24.6 0.8 copy-start.8
  25.4 0.8 copy-start.10
  29.5 35.8 %copy-start.20 = (bf16[8,2,128,128]{3,2,1,0:T(8,128)(2,1)}, bf16[8,2,128,128]{3,2,1,0:T(8,128)(2,1)S(1)}, u32[]{:S(2)}) copy-start(bf16[8,2,128,128]{3,2,1,0:T(8,128)(2,1)S(1)} %all-to-all-done.refs_4_) | copy-start | bytes 1572868
  29.5 35.8 %all-to-all-start.1 = ((bf16[8,144,512]{2,1,0:T(8,128)(2,1)}), bf16[8,144,512]{2,1,0:T(8,128)(2,1)S(1)}, u32[]{:S(2)}, u32[]{:S(2)}) async-start(bf16[8,144,512]{2,1,0:T(8,128)(2,1)} %shard_map.78), calls=%async_computation.1 | async-start | bytes 2359296 | tf_op jit(solution)/shard_map/all_to_all | solution.py:296
  33.1 15.8 %collective-permute-start.6 = (bf16[8,2,128,128]{3,2,1,0:T(8,128)(2,1)S(1)}, bf16[8,2,128,128]{3,2,1,0:T(8,128)(2,1)S(1)}, u32[]{:S(2)}, u32[]{:S(2)}) collective-permute-start(bf16[8,2,128,128]{3,2,1,0:T(8,128)(2,1)S(1)} %all-to-all-done.refs_4_), channel_id=1, source_target_pairs={{0,32},{32,64},{64,96},{96,1},{1,33},{33,65},{65,97},{97,2},{2,34}... | collective-permute-start | bytes 1572872 | tf_op jit(solution)/shard_map/ppermute | solution.py:303
  36.6 22.7 %collective-permute-start.5 = (bf16[8,2,128,128]{3,2,1,0:T(8,128)(2,1)S(1)}, bf16[8,2,128,128]{3,2,1,0:T(8,128)(2,1)S(1)}, u32[]{:S(2)}, u32[]{:S(2)}) collective-permute-start(bf16[8,2,128,128]{3,2,1,0:T(8,128)(2,1)S(1)} %all-to-all-done.refs_4_), channel_id=1, source_target_pairs={{0,64},{32,96},{64,1},{96,33},{1,65},{33,97},{65,2},{97,34},{2,66}... | collective-permute-start | bytes 1572872 | tf_op jit(solution)/shard_map/ppermute | solution.py:303
  41.4 22.3 %collective-permute-start.4 = (bf16[8,2,128,128]{3,2,1,0:T(8,128)(2,1)S(1)}, bf16[8,2,128,128]{3,2,1,0:T(8,128)(2,1)S(1)}, u32[]{:S(2)}, u32[]{:S(2)}) collective-permute-start(bf16[8,2,128,128]{3,2,1,0:T(8,128)(2,1)S(1)} %all-to-all-done.refs_4_), channel_id=1, source_target_pairs={{0,96},{32,1},{64,33},{96,65},{1,97},{33,2},{65,34},{97,66},{2,98}... | collective-permute-start | bytes 1572872 | tf_op jit(solution)/shard_map/ppermute | solution.py:303
  44.2 19.6 %collective-permute-start.3 = (bf16[8,2,128,128]{3,2,1,0:T(8,128)(2,1)S(1)}, bf16[8,2,128,128]{3,2,1,0:T(8,128)(2,1)}, u32[]{:S(2)}, u32[]{:S(2)}) collective-permute-start(bf16[8,2,128,128]{3,2,1,0:T(8,128)(2,1)S(1)} %all-to-all-done.refs_4_), channel_id=1, source_target_pairs={{0,1},{32,33},{64,65},{96,97},{1,2},{33,34},{65,66},{97,98},{2,3},... | collective-permute-start | bytes 1572872 | tf_op jit(solution)/shard_map/ppermute | solution.py:303
  48.8 16.5 %copy-start.21 = (bf16[8,2,128,128]{3,2,1,0:T(8,128)(2,1)}, bf16[8,2,128,128]{3,2,1,0:T(8,128)(2,1)S(1)}, u32[]{:S(2)}) copy-start(bf16[8,2,128,128]{3,2,1,0:T(8,128)(2,1)S(1)} %collective-permute-done.6.refs_3_) | copy-start | bytes 1572868
  59.3 6.0 %copy-start.22 = (bf16[8,2,128,128]{3,2,1,0:T(8,128)(2,1)}, bf16[8,2,128,128]{3,2,1,0:T(8,128)(2,1)S(1)}, u32[]{:S(2)}) copy-start(bf16[8,2,128,128]{3,2,1,0:T(8,128)(2,1)S(1)} %collective-permute-done.5.refs_2_) | copy-start | bytes 1572868
  63.7 1.6 %copy-start.23 = (bf16[8,2,128,128]{3,2,1,0:T(8,128)(2,1)}, bf16[8,2,128,128]{3,2,1,0:T(8,128)(2,1)S(1)}, u32[]{:S(2)}) copy-start(bf16[8,2,128,128]{3,2,1,0:T(8,128)(2,1)S(1)} %collective-permute-done.4.refs_1_) | copy-start | bytes 1572868
  65.3 1.1 copy-start
  72.1 23.4 %all-to-all-start.2 = ((bf16[8,64,512]{2,1,0:T(8,128)(2,1)}), bf16[8,64,512]{2,1,0:T(8,128)(2,1)S(1)}, u32[]{:S(2)}, u32[]{:S(2)}) async-start(bf16[8,64,512]{2,1,0:T(8,128)(2,1)} %get-tuple-element.27), calls=%async_computation.2 | async-start | bytes 1048576 | tf_op jit(solution)/shard_map/all_to_all | solution.py:296
  77.8 1.3 copy-start.1
  79.1 1.7 %copy-start.16 = (bf16[5120,256]{1,0:T(8,128)(2,1)S(1)}, bf16[5120,256]{1,0:T(8,128)(2,1)}, u32[]{:S(2)}) copy-start(bf16[5120,256]{1,0:T(8,128)(2,1)} %get-tuple-element.26.v_all) | copy-start | bytes 7864324
  80.8 1.3 copy-start.18
  82.2 24.1 %copy-start.2 = (bf16[8,144,512]{2,1,0:T(8,128)(2,1)S(1)}, bf16[8,144,512]{2,1,0:T(8,128)(2,1)}, u32[]{:S(2)}) copy-start(bf16[8,144,512]{2,1,0:T(8,128)(2,1)} %copy-done) | copy-start | bytes 3538948
  95.4 27.1 %all-to-all-start.3 = ((bf16[8,128,256]{2,1,0:T(8,128)(2,1)}), bf16[8,128,256]{2,1,0:T(8,128)(2,1)S(1)}, u32[]{:S(2)}, u32[]{:S(2)}) async-start(bf16[8,128,256]{2,1,0:T(8,128)(2,1)} %shard_map.81), calls=%async_computation.3 | async-start | bytes 1048576 | tf_op jit(solution)/shard_map/all_to_all | solution.py:296
  102.6 40.9 %copy-start.14 = (f32[4096]{0:T(1024)S(1)}, f32[4096]{0:T(1024)}, u32[]{:S(2)}) copy-start(f32[4096]{0:T(1024)} %param.10) | copy-start | bytes 49156
  102.6 19.9 %collective-permute-start.8 = (bf16[8,64,512]{2,1,0:T(8,128)(2,1)S(1)}, bf16[8,64,512]{2,1,0:T(8,128)(2,1)S(1)}, u32[]{:S(2)}, u32[]{:S(2)}) collective-permute-start(bf16[8,64,512]{2,1,0:T(8,128)(2,1)S(1)} %all-to-all-done.2.refs_0_), channel_id=1, source_target_pairs={{0,96},{32,0},{64,32},{96,64},{1,97},{33,1},{65,33},{97,65},{2,98}... | collective-permute-start | bytes 1572872 | tf_op jit(solution)/shard_map/ppermute | solution.py:325
  106.2 16.3 %collective-permute-start.7 = (bf16[8,64,512]{2,1,0:T(8,128)(2,1)S(1)}, bf16[8,64,512]{2,1,0:T(8,128)(2,1)S(1)}, u32[]{:S(2)}, u32[]{:S(2)}) collective-permute-start(bf16[8,64,512]{2,1,0:T(8,128)(2,1)S(1)} %all-to-all-done.2.refs_0_), channel_id=1, source_target_pairs={{0,32},{32,64},{64,96},{96,0},{1,33},{33,65},{65,97},{97,1},{2,34}... | collective-permute-start | bytes 1572872 | tf_op jit(solution)/shard_map/ppermute | solution.py:325
  106.2 1.7 %copy-start.17 = (bf16[5120,256]{1,0:T(8,128)(2,1)S(1)}, bf16[5120,256]{1,0:T(8,128)(2,1)}, u32[]{:S(2)}) copy-start(bf16[5120,256]{1,0:T(8,128)(2,1)} %get-tuple-element.26.v_all) | copy-start | bytes 7864324
  108.0 1.3 copy-start.19
  122.6 21.0 %copy-start.5 = (bf16[1024,192]{0,1:T(8,128)(2,1)S(1)}, bf16[1024,192]{0,1:T(8,128)(2,1)}, u32[]{:S(2)}) copy-start(bf16[1024,192]{0,1:T(8,128)(2,1)} %param.11) | copy-start | bytes 1179652
  122.6 26.9 %all-to-all-start.4 = ((bf16[8,128,256]{2,1,0:T(8,128)(2,1)}), bf16[8,128,256]{2,1,0:T(8,128)(2,1)S(1)}, u32[]{:S(2)}, u32[]{:S(2)}) async-start(bf16[8,128,256]{2,1,0:T(8,128)(2,1)} %shard_map.80), calls=%async_computation.4 | async-start | bytes 1048576 | tf_op jit(solution)/shard_map/all_to_all | solution.py:296
  129.8 13.7 %collective-permute-start.9 = (bf16[8,64,512]{2,1,0:T(8,128)(2,1)S(1)}, bf16[8,64,512]{2,1,0:T(8,128)(2,1)S(1)}, u32[]{:S(2)}, u32[]{:S(2)}) collective-permute-start(bf16[8,64,512]{2,1,0:T(8,128)(2,1)S(1)} %all-to-all-done.2.refs_0_), channel_id=1, source_target_pairs={{0,64},{32,96},{64,0},{96,32},{1,65},{33,97},{65,1},{97,33},{2,66}... | collective-permute-start | bytes 1572872 | tf_op jit(solution)/shard_map/ppermute | solution.py:325
  143.6 1.0 copy-start.7
  144.6 1.0 copy-start.9
  145.5 1.0 copy-start.11

commit v3 on v2

--- a/solution.py
+++ b/solution.py
@@ -28,11 +28,15 @@
 CHUNK = 512
 CALLS = 2
 COEF = 1.4426950408889634 / HEAD_DIM**0.5
-VMEM_LIMIT = 20 * 2**20
-FIRST_LIMIT = 56 * 2**20
+VMEM_LIMIT = 14 * 2**20
+PACK_LIMIT = 60 * 2**20
 PLACES = ("y", "xl", "core")
 GROUPS = 4 * N_Y
 SWAP = [(0, 1), (1, 0)]
+LAID_OUT = [
+    pltpu.VMEM((REACH, 2 * HEAD_DIM), jnp.bfloat16),
+    pltpu.VMEM((REACH, 2 * HEAD_DIM), jnp.bfloat16),
+]
 
 
 def scores_of(q, k):
@@ -54,7 +58,7 @@
     return pl.pallas_call(
         pack_kv_kernel,
         out_shape=jax.ShapeDtypeStruct((KV_HEADS, 2, ROWS, HEAD_DIM), keys.dtype),
-        compiler_params=pltpu.CompilerParams(vmem_limit_bytes=VMEM_LIMIT),
+        compiler_params=pltpu.CompilerParams(vmem_limit_bytes=PACK_LIMIT),
         cost_estimate=pl.CostEstimate(flops=0, bytes_accessed=2**20, transcendentals=0),
     )(keys, values)
 
@@ -89,12 +93,12 @@
     )(mem_pos, queries)
 
 
-def first_kernel(absent_ref, q_ref, *refs):
-    pieces, (k_all, v_all, o_ref) = refs[: PRIOR + 1], refs[PRIOR + 1 :]
+def lay_out(absent_ref, pieces, k_all, v_all):
     for slot, piece in enumerate(pieces):
         for z in range(N_Z):
             at = pl.ds(slot * SPAN + z * ROWS, ROWS)
-            k_all[at, :] = piece[z, 0]
+            k_all[at, :HEAD_DIM] = piece[z, 0]
+            k_all[at, HEAD_DIM:] = piece[z, 0]
             v_all[at, :HEAD_DIM] = piece[z, 1]
             v_all[at, HEAD_DIM:] = jnp.ones((ROWS, HEAD_DIM), jnp.bfloat16)
     absent = absent_ref[0]
@@ -104,9 +108,13 @@
         def _():
             first = k_all[pl.ds(pl.multiple_of(absent * SPAN, SPAN), 16), :][:1, :]
             at = pl.ds(slot * SPAN, SPAN)
-            k_all[at, :] = jnp.broadcast_to(first, (SPAN, HEAD_DIM))
+            k_all[at, :] = jnp.broadcast_to(first, (SPAN, 2 * HEAD_DIM))
             v_all[at, :] = jnp.zeros((SPAN, 2 * HEAD_DIM), jnp.bfloat16)
 
+
+def first_kernel(absent_ref, q_ref, *refs):
+    pieces, (o_ref, k_all, v_all) = refs[: PRIOR + 1], refs[PRIOR + 1 :]
+    lay_out(absent_ref, pieces, k_all, v_all)
     extra = [q_ref[z, ROWS:].astype(jnp.float32) for z in range(N_Z)]
     q = jnp.concatenate(
         [
@@ -122,7 +130,7 @@
     peak = jnp.full((count, 1), -jnp.inf, jnp.float32)
     total = jnp.zeros((count, 2 * HEAD_DIM), jnp.float32)
     for start in (*range(WINDOW, REACH, CHUNK), *range(0, WINDOW, CHUNK)):
-        s = scores_of(q, k_all[start : start + CHUNK, :])
+        s = scores_of(q, k_all[start : start + CHUNK, :HEAD_DIM])
         key = start + lax.broadcasted_iota(jnp.int32, (1, CHUNK), 1)
         if start >= WINDOW:
             s = jnp.where(key - WINDOW <= place, s, -jnp.inf)
@@ -146,12 +154,9 @@
         first_kernel,
         in_specs=[pl.BlockSpec(memory_space=pltpu.SMEM)]
         + [pl.BlockSpec(memory_space=pltpu.VMEM)] * (PRIOR + 2),
-        out_shape=(
-            jax.ShapeDtypeStruct((REACH, HEAD_DIM), q.dtype),
-            jax.ShapeDtypeStruct((REACH, 2 * HEAD_DIM), q.dtype),
-            jax.ShapeDtypeStruct((N_Z, SPAN_MEM, GROUP_COLS), q.dtype),
-        ),
-        compiler_params=pltpu.CompilerParams(vmem_limit_bytes=FIRST_LIMIT),
+        scratch_shapes=LAID_OUT,
+        out_shape=jax.ShapeDtypeStruct((N_Z, SPAN_MEM, GROUP_COLS), q.dtype),
+        compiler_params=pltpu.CompilerParams(vmem_limit_bytes=VMEM_LIMIT),
         cost_estimate=pl.CostEstimate(
             flops=GROUP_HEADS * SPAN_MEM * REACH * HEAD_DIM * 8,
             bytes_accessed=8 * 2**20,
@@ -160,15 +165,23 @@
     )(absent, q, *pieces)
 
 
-def attend_kernel(heads, q_ref, k_all, v_all, o_ref, q_rows):
+def attend_kernel(heads, absent_ref, q_ref, *refs):
+    pieces, (o_ref, k_all, v_all, q_rows) = refs[: PRIOR + 1], refs[PRIOR + 1 :]
     step = pl.program_id(0)
+
+    @pl.when(step == 0)
+    def _():
+        lay_out(absent_ref, pieces, k_all, v_all)
+
     blocks = TILE // ROWS
     count = heads * TILE
     for h in range(heads):
         for b in range(blocks):
-            q_rows[h * TILE + b * ROWS : h * TILE + (b + 1) * ROWS, :] = q_ref[
-                b, :ROWS, h * HEAD_DIM : (h + 1) * HEAD_DIM
-            ]
+            at = slice(h * TILE + b * ROWS, h * TILE + (b + 1) * ROWS)
+            scaled = q_ref[b, :ROWS, h * HEAD_DIM : (h + 1) * HEAD_DIM].astype(jnp.float32) * COEF
+            leading = scaled.astype(jnp.bfloat16)
+            q_rows[at, :HEAD_DIM] = leading
+            q_rows[at, HEAD_DIM:] = (scaled - leading.astype(jnp.float32)).astype(jnp.bfloat16)
     q = q_rows[...]
     start = step * TILE
 
@@ -182,7 +195,7 @@
     newest = scores_of(q, window(k_all, WINDOW, TILE)).reshape(heads, TILE, TILE)
     s = jnp.where(own, newest, oldest).reshape(count, TILE)
     peak = jnp.max(s, axis=1, keepdims=True)
-    p = jnp.exp2(s * COEF - peak * COEF).astype(jnp.bfloat16).reshape(heads, TILE, TILE)
+    p = jnp.exp2(s - peak).astype(jnp.bfloat16).reshape(heads, TILE, TILE)
     zero = jnp.zeros((), jnp.bfloat16)
     total = mix(jnp.where(own, p, zero).reshape(count, TILE), window(v_all, WINDOW, TILE))
     total += mix(jnp.where(own, zero, p).reshape(count, TILE), window(v_all, 0, TILE))
@@ -191,8 +204,8 @@
         size = min(CHUNK, WINDOW - offset)
         s = scores_of(q, window(k_all, offset, size))
         higher = jnp.maximum(peak, jnp.max(s, axis=1, keepdims=True))
-        fade = jnp.exp2(peak * COEF - higher * COEF)
-        p = jnp.exp2(s * COEF - higher * COEF).astype(jnp.bfloat16)
+        fade = jnp.exp2(peak - higher)
+        p = jnp.exp2(s - higher).astype(jnp.bfloat16)
         total = total * fade + mix(p, window(v_all, offset, size))
         peak = higher
         offset += size
@@ -204,7 +217,7 @@
             ]
 
 
-def attend(q, k_all, v_all, part):
+def attend(q, pieces, absent, part):
     heads = GROUP_HEADS // CALLS
     cols = heads * HEAD_DIM
     blocks = TILE // ROWS
@@ -212,12 +225,12 @@
         functools.partial(attend_kernel, heads),
         grid=(SPAN // TILE,),
         in_specs=[
+            pl.BlockSpec(memory_space=pltpu.SMEM),
             pl.BlockSpec((blocks, ROWS + EXTRA, cols), lambda i: (i, 0, part)),
-            pl.BlockSpec((REACH, HEAD_DIM), lambda i: (0, 0)),
-            pl.BlockSpec((REACH, 2 * HEAD_DIM), lambda i: (0, 0)),
-        ],
+        ]
+        + [pl.BlockSpec(memory_space=pltpu.VMEM)] * (PRIOR + 1),
         out_specs=pl.BlockSpec((blocks, ROWS, cols), lambda i: (i, 0, 0)),
-        scratch_shapes=[pltpu.VMEM((heads * TILE, HEAD_DIM), jnp.bfloat16)],
+        scratch_shapes=LAID_OUT + [pltpu.VMEM((heads * TILE, 2 * HEAD_DIM), jnp.bfloat16)],
         out_shape=jax.ShapeDtypeStruct((N_Z, ROWS, cols), q.dtype),
         compiler_params=pltpu.CompilerParams(vmem_limit_bytes=VMEM_LIMIT),
         cost_estimate=pl.CostEstimate(
@@ -225,7 +238,7 @@
             bytes_accessed=4 * 2**20,
             transcendentals=heads * SPAN * WINDOW,
         ),
-    )(q, k_all, v_all)
+    )(absent, q, *pieces)
 
 
 def unpack_kernel(*refs):
@@ -247,27 +260,29 @@
 
 
 def summary_kernel(place_ref, *refs):
-    rows, gain_ref, weights = refs[:N_Y], refs[N_Y], refs[N_Y + 1 : N_Y + 5]
-    o_ref, normed = refs[N_Y + 5 :]
+    rows, gain_ref, weights = refs[: N_Y + 1], refs[N_Y + 1], refs[N_Y + 2 : N_Y + 6]
+    o_ref, normed = refs[N_Y + 6 :]
+    blocks = [[rows[0]], [rows[1]], rows[2:4], [rows[4]]]
     y, xl, core = place_ref[0], place_ref[1], place_ref[2]
-    for back, rows_ref in enumerate(rows):
+    for back, block in enumerate(blocks):
+        block = [ref[z] for ref in block for z in range(ref.shape[0])]
         squares = jnp.zeros((SPAN_MEM, 1), jnp.float32)
         for z in range(N_Z):
-            picked = rows_ref[z].astype(jnp.float32)
+            picked = block[z].astype(jnp.float32)
             squares += jnp.sum(picked * picked, axis=1, keepdims=True)
         factor = lax.rsqrt(squares / D + 1e-05)
         at = pl.ds(pl.multiple_of((y - back + N_Y) % N_Y * SPAN_MEM, SPAN_MEM), SPAN_MEM)
         for z in range(N_Z):
             gain = gain_ref[:, z * GROUP_COLS : (z + 1) * GROUP_COLS]
-            picked = rows_ref[z].astype(jnp.float32)
+            picked = block[z].astype(jnp.float32)
             normed[z, at, :] = (picked * factor * gain).astype(jnp.bfloat16)
     total = jnp.zeros(o_ref.shape, jnp.float32)
-    half = N_Z // 4
+    per = N_Z // 4
     for i, w_ref in enumerate(weights):
         tp = (xl + i // 2) % 2 * 2 + (core + i % 2) % 2
-        for k in range(half):
+        for k in range(per):
             cols = slice(k * GROUP_COLS, (k + 1) * GROUP_COLS)
-            total += scores_of(w_ref[:, cols], normed[tp * half + k])
+            total += scores_of(w_ref[:, cols], normed[tp * per + k])
     o_ref[...] = total.astype(jnp.bfloat16)
 
 
@@ -276,7 +291,7 @@
     vmem = pl.BlockSpec(memory_space=pltpu.VMEM)
     return pl.pallas_call(
         summary_kernel,
-        in_specs=[pl.BlockSpec(memory_space=pltpu.SMEM)] + [vmem] * (N_Y + 5),
+        in_specs=[pl.BlockSpec(memory_space=pltpu.SMEM)] + [vmem] * (N_Y + 6),
         scratch_shapes=[pltpu.VMEM((N_Z, N_Y * SPAN_MEM, GROUP_COLS), jnp.bfloat16)],
         out_shape=jax.ShapeDtypeStruct((cols, N_Y * SPAN_MEM), jnp.bfloat16),
         compiler_params=pltpu.CompilerParams(vmem_limit_bytes=VMEM_LIMIT),
@@ -313,24 +328,28 @@
     weight, _ = together(summary_weight.T, kv)
     across = lax.ppermute(weight, "xl", SWAP)
     beside = lax.ppermute(weight, "core", SWAP)
+    own, q, across, beside = together(own, pack_q(mem_pos, queries), across, beside)
     weights = [weight, beside, across, lax.ppermute(across, "core", SWAP)]
-    own, q, weights = together(own, pack_q(mem_pos, queries), weights)
     q = exchange(q, "z")
     pieces = [from_group_behind(own, back) for back in range(PRIOR, 0, -1)] + [own]
-    k_all, v_all, picked = attend_first(q, pieces, absent)
+    q, weights = together(q, weights)
+    picked = attend_first(q, pieces, absent)
 
     picked = exchange(picked, "z")
-    out, picked = together(attend(q, k_all, v_all, 0), picked)
-    rows = [picked] + [
-        lax.ppermute(picked, "y", [(i, (i + back) % N_Y) for i in range(N_Y)])
-        for back in range(1, N_Y)
-    ]
+    out, picked = together(attend(q, pieces, absent, 0), picked)
+    def from_y_behind(a, back):
+        return lax.ppermute(a, "y", [(i, (i + back) % N_Y) for i in range(N_Y)])
+
+    low = picked[: N_Z // 2]
+    next_to = [from_y_behind(picked, 1), from_y_behind(picked, 3), from_y_behind(low, 2)]
     sent = [exchange(out, "z")]
     for part in range(1, CALLS):
-        out, sent = together(attend(q, k_all, v_all, part), sent)
+        out, sent = together(attend(q, pieces, absent, part), sent)
         if part == CALLS - 1:
-            out, rows[1], rows[3] = together(out, rows[1], rows[3])
+            out, next_to, picked = together(out, next_to, picked)
         sent = sent + [exchange(out, "z")]
+    high = picked[N_Z // 2 :]
+    rows = [picked, next_to[0], next_to[2], from_y_behind(high, 2), next_to[1]]
     summary = summarize(jnp.stack((y, xl, core)), rows, norm_gain, weights)
     sent, summary = together(sent, summary)
     return unpack(sent), summary.T

time: 151 us -> 145 us (0.960)
  local copies, waits for them, and re-layouts: 15.1 us -> 3.55 us
  waiting for transfers between devices: 42 us -> 47.1 us
  starting transfers between devices: 53.6 us -> 49.9 us
  Pallas kernels: 39 us -> 42.6 us
    all_to_all x5, waiting for transfers between devices: 4.87 us -> 26.9 us  [exchange(): return lax.all_to_all(a, axis, split_axis=0, concat_axis=0, tiled=True)]
    ppermute x4, waiting for transfers between devices: 15.9 us -> 0.01 us  [from_group_behind(): lax.ppermute(a, PLACES, [(index(g - back), index(g)) for g in range(back,...]
    unnamed x48 -> x26, local copies, waits for them, and re-layouts: 15.1 us -> 2.81 us
    all_to_all x5, starting transfers between devices: 32.2 us -> 28.3 us  [exchange(): return lax.all_to_all(a, axis, split_axis=0, concat_axis=0, tiled=True)]
    pallas_call x2, Pallas kernels: 26.5 us -> 28.6 us  [attend(): pl.pallas_call(functools.partial(attend_kernel, heads), grid=(SPAN // TIL...]
    ppermute x1, waiting for transfers between devices: 9.37 us -> 7.63 us  [on_device(): across = lax.ppermute(weight, 'xl', SWAP)]
    ppermute x1, waiting for transfers between devices: 0.01 us -> 1.72 us  [on_device(): weights = [weight, beside, across, lax.ppermute(across, 'core', SWAP)]]
    ppermute x3 -> x4, waiting for transfers between devices: 11.9 us -> 10.9 us  [from_y_behind(): return lax.ppermute(a, 'y', [(i, (i + back) % N_Y) for i in range(N_Y)])]
  transfers between devices with their start and end apart: 15 -> 16, of which waited for: 7 -> 9; matrix products, arithmetic and copies ran while one was open for 0% -> 1% of each run, Pallas kernels for 21% -> 24%
where the time goes in v3:
time: 145 us; the launch traced here: 144 us
  starting transfers between devices  49.9 us (34%)
  waiting for transfers between devices  47.1 us (32%)
  Pallas kernels  42.6 us (29%)
  local copies, waits for them, and re-layouts  3.55 us (2%)
    pallas_call x2, Pallas kernels, attend(): pl.pallas_call(functools.partial(attend_kernel, heads), grid=(SPAN // TIL...  28.6 us
    all_to_all x5, starting transfers between devices, exchange(): return lax.all_to_all(a, axis, split_axis=0, concat_axis=0, tiled=True)  28.3 us
    all_to_all x5, waiting for transfers between devices, exchange(): return lax.all_to_all(a, axis, split_axis=0, concat_axis=0, tiled=True)  26.9 us
    ppermute x4, starting transfers between devices, from_group_behind(): lax.ppermute(a, PLACES, [(index(g - back), index(g)) for g in range(back,...  14.7 us
    ppermute x4, waiting for transfers between devices, from_y_behind(): return lax.ppermute(a, 'y', [(i, (i + back) % N_Y) for i in range(N_Y)])  10.9 us
    ppermute x1, waiting for transfers between devices, on_device(): across = lax.ppermute(weight, 'xl', SWAP)  7.63 us
    pallas_call x1, Pallas kernels, attend_first(): pl.pallas_call(first_kernel, in_specs=[pl.BlockSpec(memory_space=pltpu.SM...  5.46 us
    ppermute x4, starting transfers between devices, from_y_behind(): return lax.ppermute(a, 'y', [(i, (i + back) % N_Y) for i in range(N_Y)])  5.44 us
  transfers between devices with their start and end apart: 16, of which 9 were waited for; matrix products, arithmetic and copies ran while one was open for 1% of the time, Pallas kernels for 24%

profile of v3, /device:TPU:4, one launch (start us, length us, event | category | flops | bytes accessed | tf_op | source)
XLA Modules:
  0.0 143.9 jit_solution(13356205033641263525)
XLA Ops:
  0.6 0.0 copy-start.1
  0.7 2.0 %shard_map.77 = bf16[8,2,128,128]{3,2,1,0:T(8,128)(2,1)} custom-call(bf16[128,1024]{1,0:T(8,128)(2,1)} %k_ref.1, bf16[128,1024]{1,0:T(8,128)(2,1)} %v_ref.1), custom_call_target="tpu_custom_call" | custom-call | bytes 1048576 | tf_op jit(solution)/shard_map/pallas_call | solution.py:58
  2.7 8.5 %all-to-all-start = ((bf16[8,2,128,128]{3,2,1,0:T(8,128)(2,1)}), bf16[8,2,128,128]{3,2,1,0:T(8,128)(2,1)S(1)}, u32[]{:S(2)}, u32[]{:S(2)}) async-start(bf16[8,2,128,128]{3,2,1,0:T(8,128)(2,1)} %shard_map.77), calls=%async_computation | async-start | bytes 1048576 | tf_op jit(solution)/shard_map/all_to_all | solution.py:311
  11.2 0.1 collective-permute-start.1
  11.3 1.3 collective-permute-start
  12.5 0.0 copy-done.10
  12.5 1.9 %shard_map.78 = bf16[8,144,512]{2,1,0:T(8,128)(2,1)} custom-call(s32[8]{0:T(128)S(1)} %copy-done.10, bf16[128,4096]{1,0:T(8,128)(2,1)S(1)} %copy-done), custom_call_target="tpu_custom_call" | custom-call | flops 134217728 | bytes 2097152 | tf_op jit(solution)/shard_map/pallas_call | solution.py:84
  14.4 0.0 collective-permute-done.1.refs_7_
  14.4 0.7 copy-done.3
  15.2 7.6 %collective-permute-done.refs_8_ = bf16[192,1024]{1,0:T(8,128)(2,1)S(1)} collective-permute-done((bf16[192,1024]{1,0:T(8,128)(2,1)S(1)}, bf16[192,1024]{1,0:T(8,128)(2,1)S(1)}, u32[]{:S(2)}, u32[]{:S(2)}) %collective-permute-start) | collective-permute-done | bytes 393248 | tf_op jit(solution)/shard_map/ppermute | solution.py:329
  22.8 5.9 %all-to-all-done.refs_4_ = bf16[8,2,128,128]{3,2,1,0:T(8,128)(2,1)S(1)} async-done(((bf16[8,2,128,128]{3,2,1,0:T(8,128)(2,1)}), bf16[8,2,128,128]{3,2,1,0:T(8,128)(2,1)S(1)}, u32[]{:S(2)}, u32[]{:S(2)}) %all-to-all-start) | async-done | bytes 524320 | tf_op jit(solution)/shard_map/all_to_all | solution.py:311
  28.6 3.6 %all-to-all-start.1 = ((bf16[8,144,512]{2,1,0:T(8,128)(2,1)}), bf16[8,144,512]{2,1,0:T(8,128)(2,1)S(1)}, u32[]{:S(2)}, u32[]{:S(2)}) async-start(bf16[8,144,512]{2,1,0:T(8,128)(2,1)} %shard_map.78), calls=%async_computation.1 | async-start | bytes 2359296 | tf_op jit(solution)/shard_map/all_to_all | solution.py:311
  32.2 3.5 %collective-permute-start.6 = (bf16[8,2,128,128]{3,2,1,0:T(8,128)(2,1)S(1)}, bf16[8,2,128,128]{3,2,1,0:T(8,128)(2,1)S(1)}, u32[]{:S(2)}, u32[]{:S(2)}) collective-permute-start(bf16[8,2,128,128]{3,2,1,0:T(8,128)(2,1)S(1)} %all-to-all-done.refs_4_), channel_id=1, source_target_pairs={{0,32},{32,64},{64,96},{96,1},{1,33},{33,65},{65,97},{97,2},{2,34}... | collective-permute-start | bytes 1572872 | tf_op jit(solution)/shard_map/ppermute | solution.py:318
  35.7 5.6 %collective-permute-start.5 = (bf16[8,2,128,128]{3,2,1,0:T(8,128)(2,1)S(1)}, bf16[8,2,128,128]{3,2,1,0:T(8,128)(2,1)}, u32[]{:S(2)}, u32[]{:S(2)}) collective-permute-start(bf16[8,2,128,128]{3,2,1,0:T(8,128)(2,1)S(1)} %all-to-all-done.refs_4_), channel_id=1, source_target_pairs={{0,64},{32,96},{64,1},{96,33},{1,65},{33,97},{65,2},{97,34},{2,66}... | collective-permute-start | bytes 1572872 | tf_op jit(solution)/shard_map/ppermute | solution.py:318
  41.3 2.6 %collective-permute-start.4 = (bf16[8,2,128,128]{3,2,1,0:T(8,128)(2,1)S(1)}, bf16[8,2,128,128]{3,2,1,0:T(8,128)(2,1)}, u32[]{:S(2)}, u32[]{:S(2)}) collective-permute-start(bf16[8,2,128,128]{3,2,1,0:T(8,128)(2,1)S(1)} %all-to-all-done.refs_4_), channel_id=1, source_target_pairs={{0,96},{32,1},{64,33},{96,65},{1,97},{33,2},{65,34},{97,66},{2,98}... | collective-permute-start | bytes 1572872 | tf_op jit(solution)/shard_map/ppermute | solution.py:318
  43.9 3.0 %collective-permute-start.3 = (bf16[8,2,128,128]{3,2,1,0:T(8,128)(2,1)S(1)}, bf16[8,2,128,128]{3,2,1,0:T(8,128)(2,1)}, u32[]{:S(2)}, u32[]{:S(2)}) collective-permute-start(bf16[8,2,128,128]{3,2,1,0:T(8,128)(2,1)S(1)} %all-to-all-done.refs_4_), channel_id=1, source_target_pairs={{0,1},{32,33},{64,65},{96,97},{1,2},{33,34},{65,66},{97,98},{2,3},... | collective-permute-start | bytes 1572872 | tf_op jit(solution)/shard_map/ppermute | solution.py:318
  47.0 0.0 collective-permute-start.2
  47.0 0.0 copy-done.5
  47.0 1.7 %collective-permute-done.2.refs_9_ = bf16[192,1024]{1,0:T(8,128)(2,1)S(1)} collective-permute-done((bf16[192,1024]{1,0:T(8,128)(2,1)S(1)}, bf16[192,1024]{1,0:T(8,128)(2,1)S(1)}, u32[]{:S(2)}, u32[]{:S(2)}) %collective-permute-start.2) | collective-permute-done | bytes 393248 | tf_op jit(solution)/shard_map/ppermute | solution.py:332
  48.7 15.5 %all-to-all-done.1.q_ref = bf16[8,144,512]{2,1,0:T(8,128)(2,1)S(1)} async-done(((bf16[8,144,512]{2,1,0:T(8,128)(2,1)}), bf16[8,144,512]{2,1,0:T(8,128)(2,1)S(1)}, u32[]{:S(2)}, u32[]{:S(2)}) %all-to-all-start.1) | async-done | bytes 1179680 | tf_op jit(solution)/shard_map/all_to_all | solution.py:311
  64.2 0.0 collective-permute-done.6.refs_3_
  64.2 0.0 collective-permute-done.5.refs_2_
  64.2 0.0 collective-permute-done.4.refs_1_
  64.2 0.0 collective-permute-done.3.refs_0_
  64.2 5.5 %shard_map.81 = bf16[8,64,512]{2,1,0:T(8,128)(2,1)} custom-call(s32[1]{0:T(128)} %bitcast.absent_ref, bf16[8,144,512]{2,1,0:T(8,128)(2,1)S(1)} %all-to-all-done.1.q_ref, bf16[8,2,128,128]{3,2,1,0:T(8,128)(2,1)} %collective-permute-done.3.refs_0_, bf16[8,2,128,128]{3,2,1,0:T(8,128)(2,1)} %collective-permute-done.4.refs_1_, ...), custom_call_target="tpu_custom_call" | custom-call | flops 1342177280 | bytes 8388608 | tf_op jit(solution)/shard_map/pallas_call | solution.py:153
  69.7 5.6 %all-to-all-start.2 = ((bf16[8,64,512]{2,1,0:T(8,128)(2,1)}), bf16[8,64,512]{2,1,0:T(8,128)(2,1)S(1)}, u32[]{:S(2)}, u32[]{:S(2)}) async-start(bf16[8,64,512]{2,1,0:T(8,128)(2,1)} %shard_map.81), calls=%async_computation.2 | async-start | bytes 1048576 | tf_op jit(solution)/shard_map/all_to_all | solution.py:311
  75.2 14.3 %shard_map.80 = bf16[8,128,256]{2,1,0:T(8,128)(2,1)} custom-call(s32[1]{0:T(128)} %bitcast.absent_ref, bf16[8,144,512]{2,1,0:T(8,128)(2,1)S(1)} %all-to-all-done.1.q_ref, bf16[8,2,128,128]{3,2,1,0:T(8,128)(2,1)} %collective-permute-done.3.refs_0_, bf16[8,2,128,128]{3,2,1,0:T(8,128)(2,1)} %collective-permute-done.4.refs_1_, ...), custom_call_target="tpu_custom_call" | custom-call | flops 8589934592 | bytes 4194304 | tf_op jit(solution)/shard_map/pallas_call | solution.py:224
  89.5 3.3 %all-to-all-done.2.refs_0_ = bf16[8,64,512]{2,1,0:T(8,128)(2,1)S(1)} async-done(((bf16[8,64,512]{2,1,0:T(8,128)(2,1)}), bf16[8,64,512]{2,1,0:T(8,128)(2,1)S(1)}, u32[]{:S(2)}, u32[]{:S(2)}) %all-to-all-start.2) | async-done | bytes 524320 | tf_op jit(solution)/shard_map/all_to_all | solution.py:311
  92.9 3.9 %all-to-all-start.3 = ((bf16[8,128,256]{2,1,0:T(8,128)(2,1)}), bf16[8,128,256]{2,1,0:T(8,128)(2,1)S(1)}, u32[]{:S(2)}, u32[]{:S(2)}) async-start(bf16[8,128,256]{2,1,0:T(8,128)(2,1)} %shard_map.80), calls=%async_computation.3 | async-start | bytes 1048576 | tf_op jit(solution)/shard_map/all_to_all | solution.py:311
  96.7 0.7 slice.6
  97.5 3.4 %collective-permute-start.8 = (bf16[8,64,512]{2,1,0:T(8,128)(2,1)S(1)}, bf16[8,64,512]{2,1,0:T(8,128)(2,1)S(1)}, u32[]{:S(2)}, u32[]{:S(2)}) collective-permute-start(bf16[8,64,512]{2,1,0:T(8,128)(2,1)S(1)} %all-to-all-done.2.refs_0_), channel_id=1, source_target_pairs={{0,96},{32,0},{64,32},{96,64},{1,97},{33,1},{65,33},{97,65},{2,98}... | collective-permute-start | bytes 1572872 | tf_op jit(solution)/shard_map/ppermute | solution.py:341
  100.9 0.0 collective-permute-start.7
  100.9 1.5 %collective-permute-start.9 = (bf16[4,64,512]{2,1,0:T(8,128)(2,1)}, bf16[4,64,512]{2,1,0:T(8,128)(2,1)S(1)}, u32[]{:S(2)}, u32[]{:S(2)}) collective-permute-start(bf16[4,64,512]{2,1,0:T(8,128)(2,1)} %slice.6), channel_id=1, source_target_pairs={{0,64},{32,96},{64,0},{96,32},{1,65},{33,97},{65,1},{97,33},{2,66}... | collective-permute-start | bytes 786440 | tf_op jit(solution)/shard_map/ppermute | solution.py:341
  102.4 1.0 copy-done.12
  103.4 14.3 %shard_map.79 = bf16[8,128,256]{2,1,0:T(8,128)(2,1)} custom-call(s32[1]{0:T(128)} %bitcast.absent_ref, bf16[8,144,512]{2,1,0:T(8,128)(2,1)S(1)} %all-to-all-done.1.q_ref, bf16[8,2,128,128]{3,2,1,0:T(8,128)(2,1)} %collective-permute-done.3.refs_0_, bf16[8,2,128,128]{3,2,1,0:T(8,128)(2,1)} %collective-permute-done.4.refs_1_, ...), custom_call_target="tpu_custom_call" | custom-call | flops 8589934592 | bytes 4194304 | tf_op jit(solution)/shard_map/pallas_call | solution.py:224
  117.7 0.0 all-to-all-done.3.refs_0_
  117.7 2.1 %collective-permute-done.9.refs_2_ = bf16[4,64,512]{2,1,0:T(8,128)(2,1)S(1)} collective-permute-done((bf16[4,64,512]{2,1,0:T(8,128)(2,1)}, bf16[4,64,512]{2,1,0:T(8,128)(2,1)S(1)}, u32[]{:S(2)}, u32[]{:S(2)}) %collective-permute-start.9) | collective-permute-done | bytes 262176 | tf_op jit(solution)/shard_map/ppermute | solution.py:341
  119.8 0.0 collective-permute-done.8.refs_4_
  119.8 1.5 %collective-permute-done.7.refs_1_ = bf16[8,64,512]{2,1,0:T(8,128)(2,1)} collective-permute-done((bf16[8,64,512]{2,1,0:T(8,128)(2,1)S(1)}, bf16[8,64,512]{2,1,0:T(8,128)(2,1)}, u32[]{:S(2)}, u32[]{:S(2)}) %collective-permute-start.7) | collective-permute-done | bytes 524320 | tf_op jit(solution)/shard_map/ppermute | solution.py:341
  121.3 6.8 %all-to-all-start.4 = ((bf16[8,128,256]{2,1,0:T(8,128)(2,1)}), bf16[8,128,256]{2,1,0:T(8,128)(2,1)S(1)}, u32[]{:S(2)}, u32[]{:S(2)}) async-start(bf16[8,128,256]{2,1,0:T(8,128)(2,1)} %shard_map.79), calls=%async_computation.4 | async-start | bytes 1048576 | tf_op jit(solution)/shard_map/all_to_all | solution.py:311
  128.1 0.6 collective-permute-start.10
  128.7 0.1 pad_add_fusion.place_ref
  128.8 7.3 %collective-permute-done.10.refs_3_ = bf16[4,64,512]{2,1,0:T(8,128)(2,1)S(1)} collective-permute-done((bf16[4,64,512]{2,1,0:T(8,128)(2,1)S(1)}, bf16[4,64,512]{2,1,0:T(8,128)(2,1)S(1)}, u32[]{:S(2)}, u32[]{:S(2)}) %collective-permute-start.10) | collective-permute-done | bytes 262176 | tf_op jit(solution)/shard_map/ppermute | solution.py:341
  136.1 0.0 copy-done.2
  136.1 1.0 copy-done.8
  137.1 3.5 %shard_map.82 = bf16[192,256]{1,0:T(8,128)(2,1)} custom-call(s32[3]{0:T(128)S(1)} %pad_add_fusion.place_ref, bf16[8,64,512]{2,1,0:T(8,128)(2,1)S(1)} %all-to-all-done.2.refs_0_, bf16[8,64,512]{2,1,0:T(8,128)(2,1)} %collective-permute-done.7.refs_1_, bf16[4,64,512]{2,1,0:T(8,128)(2,1)S(1)} %collective-permute-done.9.refs_2_, ...), custom_call_target="tpu_custom_call" | custom-call | flops 402653184 | bytes 4194304 | tf_op jit(solution)/shard_map/pallas_call | solution.py:292
  140.7 2.2 %all-to-all-done.4.refs_1_ = bf16[8,128,256]{2,1,0:T(8,128)(2,1)S(1)} async-done(((bf16[8,128,256]{2,1,0:T(8,128)(2,1)}), bf16[8,128,256]{2,1,0:T(8,128)(2,1)S(1)}, u32[]{:S(2)}, u32[]{:S(2)}) %all-to-all-start.4) | async-done | bytes 524320 | tf_op jit(solution)/shard_map/all_to_all | solution.py:311
  142.9 1.1 shard_map.83
  (20 shorter events, 0.1 us)
Async XLA Ops:
  0.6 10.5 %copy-start.1 = (bf16[1024,192]{0,1:T(8,128)(2,1)S(1)}, bf16[1024,192]{0,1:T(8,128)(2,1)}, u32[]{:S(2)}) copy-start(bf16[1024,192]{0,1:T(8,128)(2,1)} %param.11) | copy-start | bytes 1179652
  0.6 11.9 %copy-start.10 = (s32[8]{0:T(128)S(1)}, s32[8]{0:T(128)}, u32[]{:S(2)}) copy-start(s32[8]{0:T(128)} %pos_ref.1) | copy-start | bytes 100
  0.7 11.9 %copy-start = (bf16[128,4096]{1,0:T(8,128)(2,1)S(1)}, bf16[128,4096]{1,0:T(8,128)(2,1)}, u32[]{:S(2)}) copy-start(bf16[128,4096]{1,0:T(8,128)(2,1)} %q_ref.1) | copy-start | bytes 3145732
  2.7 26.0 %all-to-all-start = ((bf16[8,2,128,128]{3,2,1,0:T(8,128)(2,1)}), bf16[8,2,128,128]{3,2,1,0:T(8,128)(2,1)S(1)}, u32[]{:S(2)}, u32[]{:S(2)}) async-start(bf16[8,2,128,128]{3,2,1,0:T(8,128)(2,1)} %shard_map.77), calls=%async_computation | async-start | bytes 1048576 | tf_op jit(solution)/shard_map/all_to_all | solution.py:311
  11.2 3.3 %collective-permute-start.1 = (bf16[192,1024]{1,0:T(8,128)(2,1)S(1)}, bf16[192,1024]{1,0:T(8,128)(2,1)S(1)}, u32[]{:S(2)}, u32[]{:S(2)}) collective-permute-start(bf16[192,1024]{1,0:T(8,128)(2,1)S(1)} %bitcast.7), channel_id=1, source_target_pairs={{0,1},{1,0},{2,3},{3,2},{4,5},{5,4},{6,7},{7,6},{8,9},{9,8},{10,11... | collective-permute-start | bytes 1179656 | tf_op jit(solution)/shard_map/ppermute | solution.py:330
  11.3 11.5 %collective-permute-start = (bf16[192,1024]{1,0:T(8,128)(2,1)S(1)}, bf16[192,1024]{1,0:T(8,128)(2,1)S(1)}, u32[]{:S(2)}, u32[]{:S(2)}) collective-permute-start(bf16[192,1024]{1,0:T(8,128)(2,1)S(1)} %bitcast.8), channel_id=1, source_target_pairs={{0,2},{2,0},{1,3},{3,1},{4,6},{6,4},{5,7},{7,5},{8,10},{10,8},{9,1... | collective-permute-start | bytes 1179656 | tf_op jit(solution)/shard_map/ppermute | solution.py:329
  14.4 0.7 copy-start.3
  22.8 24.2 %copy-start.5 = (bf16[192,1024]{1,0:T(8,128)(2,1)}, bf16[192,1024]{1,0:T(8,128)(2,1)S(1)}, u32[]{:S(2)}) copy-start(bf16[192,1024]{1,0:T(8,128)(2,1)S(1)} %collective-permute-done.refs_8_) | copy-start | bytes 1179652
  28.6 35.5 %all-to-all-start.1 = ((bf16[8,144,512]{2,1,0:T(8,128)(2,1)}), bf16[8,144,512]{2,1,0:T(8,128)(2,1)S(1)}, u32[]{:S(2)}, u32[]{:S(2)}) async-start(bf16[8,144,512]{2,1,0:T(8,128)(2,1)} %shard_map.78), calls=%async_computation.1 | async-start | bytes 2359296 | tf_op jit(solution)/shard_map/all_to_all | solution.py:311
  32.2 32.0 %collective-permute-start.6 = (bf16[8,2,128,128]{3,2,1,0:T(8,128)(2,1)S(1)}, bf16[8,2,128,128]{3,2,1,0:T(8,128)(2,1)S(1)}, u32[]{:S(2)}, u32[]{:S(2)}) collective-permute-start(bf16[8,2,128,128]{3,2,1,0:T(8,128)(2,1)S(1)} %all-to-all-done.refs_4_), channel_id=1, source_target_pairs={{0,32},{32,64},{64,96},{96,1},{1,33},{33,65},{65,97},{97,2},{2,34}... | collective-permute-start | bytes 1572872 | tf_op jit(solution)/shard_map/ppermute | solution.py:318
  35.7 28.4 %collective-permute-start.5 = (bf16[8,2,128,128]{3,2,1,0:T(8,128)(2,1)S(1)}, bf16[8,2,128,128]{3,2,1,0:T(8,128)(2,1)}, u32[]{:S(2)}, u32[]{:S(2)}) collective-permute-start(bf16[8,2,128,128]{3,2,1,0:T(8,128)(2,1)S(1)} %all-to-all-done.refs_4_), channel_id=1, source_target_pairs={{0,64},{32,96},{64,1},{96,33},{1,65},{33,97},{65,2},{97,34},{2,66}... | collective-permute-start | bytes 1572872 | tf_op jit(solution)/shard_map/ppermute | solution.py:318
  41.3 22.9 %collective-permute-start.4 = (bf16[8,2,128,128]{3,2,1,0:T(8,128)(2,1)S(1)}, bf16[8,2,128,128]{3,2,1,0:T(8,128)(2,1)}, u32[]{:S(2)}, u32[]{:S(2)}) collective-permute-start(bf16[8,2,128,128]{3,2,1,0:T(8,128)(2,1)S(1)} %all-to-all-done.refs_4_), channel_id=1, source_target_pairs={{0,96},{32,1},{64,33},{96,65},{1,97},{33,2},{65,34},{97,66},{2,98}... | collective-permute-start | bytes 1572872 | tf_op jit(solution)/shard_map/ppermute | solution.py:318
  43.9 20.3 %collective-permute-start.3 = (bf16[8,2,128,128]{3,2,1,0:T(8,128)(2,1)S(1)}, bf16[8,2,128,128]{3,2,1,0:T(8,128)(2,1)}, u32[]{:S(2)}, u32[]{:S(2)}) collective-permute-start(bf16[8,2,128,128]{3,2,1,0:T(8,128)(2,1)S(1)} %all-to-all-done.refs_4_), channel_id=1, source_target_pairs={{0,1},{32,33},{64,65},{96,97},{1,2},{33,34},{65,66},{97,98},{2,3},... | collective-permute-start | bytes 1572872 | tf_op jit(solution)/shard_map/ppermute | solution.py:318
  47.0 1.7 %collective-permute-start.2 = (bf16[192,1024]{1,0:T(8,128)(2,1)S(1)}, bf16[192,1024]{1,0:T(8,128)(2,1)S(1)}, u32[]{:S(2)}, u32[]{:S(2)}) collective-permute-start(bf16[192,1024]{1,0:T(8,128)(2,1)S(1)} %collective-permute-done.refs_8_), channel_id=1, source_target_pairs={{0,1},{1,0},{2,3},{3,2},{4,5},{5,4},{6,7},{7,6},{8,9},{9,8},{10,11... | collective-permute-start | bytes 1179656 | tf_op jit(solution)/shard_map/ppermute | solution.py:332
  48.7 21.0 %copy-start.7 = (bf16[192,1024]{1,0:T(8,128)(2,1)}, bf16[192,1024]{1,0:T(8,128)(2,1)S(1)}, u32[]{:S(2)}) copy-start(bf16[192,1024]{1,0:T(8,128)(2,1)S(1)} %collective-permute-done.2.refs_9_) | copy-start | bytes 1179652
  64.2 11.1 %copy-start.11 = (bf16[8,2,128,128]{3,2,1,0:T(8,128)(2,1)}, bf16[8,2,128,128]{3,2,1,0:T(8,128)(2,1)S(1)}, u32[]{:S(2)}) copy-start(bf16[8,2,128,128]{3,2,1,0:T(8,128)(2,1)S(1)} %collective-permute-done.6.refs_3_) | copy-start | bytes 1572868
  69.7 23.2 %all-to-all-start.2 = ((bf16[8,64,512]{2,1,0:T(8,128)(2,1)}), bf16[8,64,512]{2,1,0:T(8,128)(2,1)S(1)}, u32[]{:S(2)}, u32[]{:S(2)}) async-start(bf16[8,64,512]{2,1,0:T(8,128)(2,1)} %shard_map.81), calls=%async_computation.2 | async-start | bytes 1048576 | tf_op jit(solution)/shard_map/all_to_all | solution.py:311
  92.9 24.8 %all-to-all-start.3 = ((bf16[8,128,256]{2,1,0:T(8,128)(2,1)}), bf16[8,128,256]{2,1,0:T(8,128)(2,1)S(1)}, u32[]{:S(2)}, u32[]{:S(2)}) async-start(bf16[8,128,256]{2,1,0:T(8,128)(2,1)} %shard_map.80), calls=%async_computation.3 | async-start | bytes 1048576 | tf_op jit(solution)/shard_map/all_to_all | solution.py:311
  97.5 22.3 %collective-permute-start.8 = (bf16[8,64,512]{2,1,0:T(8,128)(2,1)S(1)}, bf16[8,64,512]{2,1,0:T(8,128)(2,1)S(1)}, u32[]{:S(2)}, u32[]{:S(2)}) collective-permute-start(bf16[8,64,512]{2,1,0:T(8,128)(2,1)S(1)} %all-to-all-done.2.refs_0_), channel_id=1, source_target_pairs={{0,96},{32,0},{64,32},{96,64},{1,97},{33,1},{65,33},{97,65},{2,98}... | collective-permute-start | bytes 1572872 | tf_op jit(solution)/shard_map/ppermute | solution.py:341
  100.9 20.4 %collective-permute-start.7 = (bf16[8,64,512]{2,1,0:T(8,128)(2,1)S(1)}, bf16[8,64,512]{2,1,0:T(8,128)(2,1)}, u32[]{:S(2)}, u32[]{:S(2)}) collective-permute-start(bf16[8,64,512]{2,1,0:T(8,128)(2,1)S(1)} %all-to-all-done.2.refs_0_), channel_id=1, source_target_pairs={{0,32},{32,64},{64,96},{96,0},{1,33},{33,65},{65,97},{97,1},{2,34}... | collective-permute-start | bytes 1572872 | tf_op jit(solution)/shard_map/ppermute | solution.py:341
  100.9 18.9 %collective-permute-start.9 = (bf16[4,64,512]{2,1,0:T(8,128)(2,1)}, bf16[4,64,512]{2,1,0:T(8,128)(2,1)S(1)}, u32[]{:S(2)}, u32[]{:S(2)}) collective-permute-start(bf16[4,64,512]{2,1,0:T(8,128)(2,1)} %slice.6), channel_id=1, source_target_pairs={{0,64},{32,96},{64,0},{96,32},{1,65},{33,97},{65,1},{97,33},{2,66}... | collective-permute-start | bytes 786440 | tf_op jit(solution)/shard_map/ppermute | solution.py:341
  102.3 1.0 copy-start.12
  117.7 18.4 %copy-start.2 = (bf16[1024,192]{0,1:T(8,128)(2,1)S(1)}, bf16[1024,192]{0,1:T(8,128)(2,1)}, u32[]{:S(2)}) copy-start(bf16[1024,192]{0,1:T(8,128)(2,1)} %param.11) | copy-start | bytes 1179652
  117.7 18.4 %copy-start.4 = (bf16[192,1024]{1,0:T(8,128)(2,1)S(1)}, bf16[192,1024]{1,0:T(8,128)(2,1)}, u32[]{:S(2)}) copy-start(bf16[192,1024]{1,0:T(8,128)(2,1)} %copy-done.3) | copy-start | bytes 1179652
  117.7 18.4 %copy-start.6 = (bf16[192,1024]{1,0:T(8,128)(2,1)S(1)}, bf16[192,1024]{1,0:T(8,128)(2,1)}, u32[]{:S(2)}) copy-start(bf16[192,1024]{1,0:T(8,128)(2,1)} %copy-done.5) | copy-start | bytes 1179652
  117.7 18.4 %copy-start.9 = (f32[4096]{0:T(1024)S(1)}, f32[4096]{0:T(1024)}, u32[]{:S(2)}) copy-start(f32[4096]{0:T(1024)} %param.10) | copy-start | bytes 49156
  121.3 21.6 %all-to-all-start.4 = ((bf16[8,128,256]{2,1,0:T(8,128)(2,1)}), bf16[8,128,256]{2,1,0:T(8,128)(2,1)S(1)}, u32[]{:S(2)}, u32[]{:S(2)}) async-start(bf16[8,128,256]{2,1,0:T(8,128)(2,1)} %shard_map.79), calls=%async_computation.4 | async-start | bytes 1048576 | tf_op jit(solution)/shard_map/all_to_all | solution.py:311
  128.1 8.0 %collective-permute-start.10 = (bf16[4,64,512]{2,1,0:T(8,128)(2,1)S(1)}, bf16[4,64,512]{2,1,0:T(8,128)(2,1)S(1)}, u32[]{:S(2)}, u32[]{:S(2)}) collective-permute-start(bf16[4,64,512]{2,1,0:T(8,128)(2,1)S(1)} %slice.7), channel_id=1, source_target_pairs={{0,64},{32,96},{64,0},{96,32},{1,65},{33,97},{65,1},{97,33},{2,66}... | collective-permute-start | bytes 786440 | tf_op jit(solution)/shard_map/ppermute | solution.py:341
  136.1 1.0 copy-start.8

commit v4 on v3

--- a/solution.py
+++ b/solution.py
@@ -33,6 +33,7 @@
 PLACES = ("y", "xl", "core")
 GROUPS = 4 * N_Y
 SWAP = [(0, 1), (1, 0)]
+SLOTS = (0, 2, 1, 3)
 LAID_OUT = [
     pltpu.VMEM((REACH, 2 * HEAD_DIM), jnp.bfloat16),
     pltpu.VMEM((REACH, 2 * HEAD_DIM), jnp.bfloat16),
@@ -94,7 +95,7 @@
 
 
 def lay_out(absent_ref, pieces, k_all, v_all):
-    for slot, piece in enumerate(pieces):
+    for slot, piece in zip((*SLOTS, PRIOR), pieces):
         for z in range(N_Z):
             at = pl.ds(slot * SPAN + z * ROWS, ROWS)
             k_all[at, :HEAD_DIM] = piece[z, 0]
@@ -331,7 +332,7 @@
     own, q, across, beside = together(own, pack_q(mem_pos, queries), across, beside)
     weights = [weight, beside, across, lax.ppermute(across, "core", SWAP)]
     q = exchange(q, "z")
-    pieces = [from_group_behind(own, back) for back in range(PRIOR, 0, -1)] + [own]
+    pieces = [from_group_behind(own, PRIOR - slot) for slot in SLOTS] + [own]
     q, weights = together(q, weights)
     picked = attend_first(q, pieces, absent)
 

time: 145 us -> 145 us (level)
  no operation moved by 1% of the time
where the time goes in v4:
time: 145 us; the launch traced here: 144 us
  starting transfers between devices  49.2 us (34%)
  waiting for transfers between devices  47.5 us (33%)
  Pallas kernels  42.6 us (29%)
  local copies, waits for them, and re-layouts  3.55 us (2%)
    pallas_call x2, Pallas kernels, attend(): pl.pallas_call(functools.partial(attend_kernel, heads), grid=(SPAN // TIL...  28.6 us
    all_to_all x5, starting transfers between devices, exchange(): return lax.all_to_all(a, axis, split_axis=0, concat_axis=0, tiled=True)  28.2 us
    all_to_all x5, waiting for transfers between devices, exchange(): return lax.all_to_all(a, axis, split_axis=0, concat_axis=0, tiled=True)  27.3 us
    ppermute x4, starting transfers between devices, from_group_behind(): lax.ppermute(a, PLACES, [(index(g - back), index(g)) for g in range(back,...  14.1 us
    ppermute x4, waiting for transfers between devices, from_y_behind(): return lax.ppermute(a, 'y', [(i, (i + back) % N_Y) for i in range(N_Y)])  10.9 us
    ppermute x1, waiting for transfers between devices, on_device(): across = lax.ppermute(weight, 'xl', SWAP)  7.63 us
    pallas_call x1, Pallas kernels, attend_first(): pl.pallas_call(first_kernel, in_specs=[pl.BlockSpec(memory_space=pltpu.SM...  5.46 us
    ppermute x4, starting transfers between devices, from_y_behind(): return lax.ppermute(a, 'y', [(i, (i + back) % N_Y) for i in range(N_Y)])  5.43 us
  transfers between devices with their start and end apart: 16, of which 9 were waited for; matrix products, arithmetic and copies ran while one was open for 1% of the time, Pallas kernels for 24%

profile of v4, /device:TPU:4, one launch (start us, length us, event | category | flops | bytes accessed | tf_op | source)
XLA Modules:
  0.0 143.7 jit_solution(15435461310664147109)
XLA Ops:
  0.6 0.0 copy-start.1
  0.6 0.0 copy-start.10
  0.7 0.0 copy-start
  0.7 2.0 %shard_map.77 = bf16[8,2,128,128]{3,2,1,0:T(8,128)(2,1)} custom-call(bf16[128,1024]{1,0:T(8,128)(2,1)} %k_ref.1, bf16[128,1024]{1,0:T(8,128)(2,1)} %v_ref.1), custom_call_target="tpu_custom_call" | custom-call | bytes 1048576 | tf_op jit(solution)/shard_map/pallas_call | solution.py:59
  2.7 8.5 %all-to-all-start = ((bf16[8,2,128,128]{3,2,1,0:T(8,128)(2,1)}), bf16[8,2,128,128]{3,2,1,0:T(8,128)(2,1)S(1)}, u32[]{:S(2)}, u32[]{:S(2)}) async-start(bf16[8,2,128,128]{3,2,1,0:T(8,128)(2,1)} %shard_map.77), calls=%async_computation | async-start | bytes 1048576 | tf_op jit(solution)/shard_map/all_to_all | solution.py:312
  11.2 0.1 collective-permute-start.1
  11.3 1.3 collective-permute-start
  12.5 1.9 %shard_map.78 = bf16[8,144,512]{2,1,0:T(8,128)(2,1)} custom-call(s32[8]{0:T(128)S(1)} %copy-done.10, bf16[128,4096]{1,0:T(8,128)(2,1)S(1)} %copy-done), custom_call_target="tpu_custom_call" | custom-call | flops 134217728 | bytes 2097152 | tf_op jit(solution)/shard_map/pallas_call | solution.py:85
  14.4 0.0 collective-permute-done.1.refs_7_
  14.4 0.7 copy-done.3
  15.2 7.6 %collective-permute-done.refs_8_ = bf16[192,1024]{1,0:T(8,128)(2,1)S(1)} collective-permute-done((bf16[192,1024]{1,0:T(8,128)(2,1)S(1)}, bf16[192,1024]{1,0:T(8,128)(2,1)S(1)}, u32[]{:S(2)}, u32[]{:S(2)}) %collective-permute-start) | collective-permute-done | bytes 393248 | tf_op jit(solution)/shard_map/ppermute | solution.py:330
  22.8 5.9 %all-to-all-done.refs_4_ = bf16[8,2,128,128]{3,2,1,0:T(8,128)(2,1)S(1)} async-done(((bf16[8,2,128,128]{3,2,1,0:T(8,128)(2,1)}), bf16[8,2,128,128]{3,2,1,0:T(8,128)(2,1)S(1)}, u32[]{:S(2)}, u32[]{:S(2)}) %all-to-all-start) | async-done | bytes 524320 | tf_op jit(solution)/shard_map/all_to_all | solution.py:312
  28.6 3.6 %all-to-all-start.1 = ((bf16[8,144,512]{2,1,0:T(8,128)(2,1)}), bf16[8,144,512]{2,1,0:T(8,128)(2,1)S(1)}, u32[]{:S(2)}, u32[]{:S(2)}) async-start(bf16[8,144,512]{2,1,0:T(8,128)(2,1)} %shard_map.78), calls=%async_computation.1 | async-start | bytes 2359296 | tf_op jit(solution)/shard_map/all_to_all | solution.py:312
  32.2 3.5 %collective-permute-start.6 = (bf16[8,2,128,128]{3,2,1,0:T(8,128)(2,1)S(1)}, bf16[8,2,128,128]{3,2,1,0:T(8,128)(2,1)S(1)}, u32[]{:S(2)}, u32[]{:S(2)}) collective-permute-start(bf16[8,2,128,128]{3,2,1,0:T(8,128)(2,1)S(1)} %all-to-all-done.refs_4_), channel_id=1, source_target_pairs={{0,32},{32,64},{64,96},{96,1},{1,33},{33,65},{65,97},{97,2},{2,34}... | collective-permute-start | bytes 1572872 | tf_op jit(solution)/shard_map/ppermute | solution.py:319
  35.7 4.1 %collective-permute-start.5 = (bf16[8,2,128,128]{3,2,1,0:T(8,128)(2,1)S(1)}, bf16[8,2,128,128]{3,2,1,0:T(8,128)(2,1)}, u32[]{:S(2)}, u32[]{:S(2)}) collective-permute-start(bf16[8,2,128,128]{3,2,1,0:T(8,128)(2,1)S(1)} %all-to-all-done.refs_4_), channel_id=1, source_target_pairs={{0,96},{32,1},{64,33},{96,65},{1,97},{33,2},{65,34},{97,66},{2,98}... | collective-permute-start | bytes 1572872 | tf_op jit(solution)/shard_map/ppermute | solution.py:319
  39.9 4.2 %collective-permute-start.4 = (bf16[8,2,128,128]{3,2,1,0:T(8,128)(2,1)S(1)}, bf16[8,2,128,128]{3,2,1,0:T(8,128)(2,1)}, u32[]{:S(2)}, u32[]{:S(2)}) collective-permute-start(bf16[8,2,128,128]{3,2,1,0:T(8,128)(2,1)S(1)} %all-to-all-done.refs_4_), channel_id=1, source_target_pairs={{0,64},{32,96},{64,1},{96,33},{1,65},{33,97},{65,2},{97,34},{2,66}... | collective-permute-start | bytes 1572872 | tf_op jit(solution)/shard_map/ppermute | solution.py:319
  44.1 2.2 %collective-permute-start.3 = (bf16[8,2,128,128]{3,2,1,0:T(8,128)(2,1)S(1)}, bf16[8,2,128,128]{3,2,1,0:T(8,128)(2,1)}, u32[]{:S(2)}, u32[]{:S(2)}) collective-permute-start(bf16[8,2,128,128]{3,2,1,0:T(8,128)(2,1)S(1)} %all-to-all-done.refs_4_), channel_id=1, source_target_pairs={{0,1},{32,33},{64,65},{96,97},{1,2},{33,34},{65,66},{97,98},{2,3},... | collective-permute-start | bytes 1572872 | tf_op jit(solution)/shard_map/ppermute | solution.py:319
  46.4 0.0 collective-permute-start.2
  46.4 1.7 %collective-permute-done.2.refs_9_ = bf16[192,1024]{1,0:T(8,128)(2,1)S(1)} collective-permute-done((bf16[192,1024]{1,0:T(8,128)(2,1)S(1)}, bf16[192,1024]{1,0:T(8,128)(2,1)S(1)}, u32[]{:S(2)}, u32[]{:S(2)}) %collective-permute-start.2) | collective-permute-done | bytes 393248 | tf_op jit(solution)/shard_map/ppermute | solution.py:333
  48.1 16.1 %all-to-all-done.1.q_ref = bf16[8,144,512]{2,1,0:T(8,128)(2,1)S(1)} async-done(((bf16[8,144,512]{2,1,0:T(8,128)(2,1)}), bf16[8,144,512]{2,1,0:T(8,128)(2,1)S(1)}, u32[]{:S(2)}, u32[]{:S(2)}) %all-to-all-start.1) | async-done | bytes 1179680 | tf_op jit(solution)/shard_map/all_to_all | solution.py:312
  64.2 0.0 collective-permute-done.6.refs_3_
  64.2 0.0 collective-permute-done.5.refs_2_
  64.2 0.0 collective-permute-done.4.refs_1_
  64.2 0.0 collective-permute-done.3.refs_0_
  64.2 5.5 %shard_map.81 = bf16[8,64,512]{2,1,0:T(8,128)(2,1)} custom-call(s32[1]{0:T(128)} %bitcast.absent_ref, bf16[8,144,512]{2,1,0:T(8,128)(2,1)S(1)} %all-to-all-done.1.q_ref, bf16[8,2,128,128]{3,2,1,0:T(8,128)(2,1)} %collective-permute-done.3.refs_0_, bf16[8,2,128,128]{3,2,1,0:T(8,128)(2,1)} %collective-permute-done.4.refs_1_, ...), custom_call_target="tpu_custom_call" | custom-call | flops 1342177280 | bytes 8388608 | tf_op jit(solution)/shard_map/pallas_call | solution.py:154
  69.7 5.3 %all-to-all-start.2 = ((bf16[8,64,512]{2,1,0:T(8,128)(2,1)}), bf16[8,64,512]{2,1,0:T(8,128)(2,1)S(1)}, u32[]{:S(2)}, u32[]{:S(2)}) async-start(bf16[8,64,512]{2,1,0:T(8,128)(2,1)} %shard_map.81), calls=%async_computation.2 | async-start | bytes 1048576 | tf_op jit(solution)/shard_map/all_to_all | solution.py:312
  75.0 14.3 %shard_map.80 = bf16[8,128,256]{2,1,0:T(8,128)(2,1)} custom-call(s32[1]{0:T(128)} %bitcast.absent_ref, bf16[8,144,512]{2,1,0:T(8,128)(2,1)S(1)} %all-to-all-done.1.q_ref, bf16[8,2,128,128]{3,2,1,0:T(8,128)(2,1)} %collective-permute-done.3.refs_0_, bf16[8,2,128,128]{3,2,1,0:T(8,128)(2,1)} %collective-permute-done.4.refs_1_, ...), custom_call_target="tpu_custom_call" | custom-call | flops 8589934592 | bytes 4194304 | tf_op jit(solution)/shard_map/pallas_call | solution.py:225
  89.3 3.2 %all-to-all-done.2.refs_0_ = bf16[8,64,512]{2,1,0:T(8,128)(2,1)S(1)} async-done(((bf16[8,64,512]{2,1,0:T(8,128)(2,1)}), bf16[8,64,512]{2,1,0:T(8,128)(2,1)S(1)}, u32[]{:S(2)}, u32[]{:S(2)}) %all-to-all-start.2) | async-done | bytes 524320 | tf_op jit(solution)/shard_map/all_to_all | solution.py:312
  92.5 4.0 %all-to-all-start.3 = ((bf16[8,128,256]{2,1,0:T(8,128)(2,1)}), bf16[8,128,256]{2,1,0:T(8,128)(2,1)S(1)}, u32[]{:S(2)}, u32[]{:S(2)}) async-start(bf16[8,128,256]{2,1,0:T(8,128)(2,1)} %shard_map.80), calls=%async_computation.3 | async-start | bytes 1048576 | tf_op jit(solution)/shard_map/all_to_all | solution.py:312
  96.5 0.7 slice.6
  97.3 3.4 %collective-permute-start.8 = (bf16[8,64,512]{2,1,0:T(8,128)(2,1)S(1)}, bf16[8,64,512]{2,1,0:T(8,128)(2,1)S(1)}, u32[]{:S(2)}, u32[]{:S(2)}) collective-permute-start(bf16[8,64,512]{2,1,0:T(8,128)(2,1)S(1)} %all-to-all-done.2.refs_0_), channel_id=1, source_target_pairs={{0,96},{32,0},{64,32},{96,64},{1,97},{33,1},{65,33},{97,65},{2,98}... | collective-permute-start | bytes 1572872 | tf_op jit(solution)/shard_map/ppermute | solution.py:342
  100.7 0.0 collective-permute-start.7
  100.7 1.5 %collective-permute-start.9 = (bf16[4,64,512]{2,1,0:T(8,128)(2,1)}, bf16[4,64,512]{2,1,0:T(8,128)(2,1)S(1)}, u32[]{:S(2)}, u32[]{:S(2)}) collective-permute-start(bf16[4,64,512]{2,1,0:T(8,128)(2,1)} %slice.6), channel_id=1, source_target_pairs={{0,64},{32,96},{64,0},{96,32},{1,65},{33,97},{65,1},{97,33},{2,66}... | collective-permute-start | bytes 786440 | tf_op jit(solution)/shard_map/ppermute | solution.py:342
  102.1 1.0 copy-done.12
  103.2 14.3 %shard_map.79 = bf16[8,128,256]{2,1,0:T(8,128)(2,1)} custom-call(s32[1]{0:T(128)} %bitcast.absent_ref, bf16[8,144,512]{2,1,0:T(8,128)(2,1)S(1)} %all-to-all-done.1.q_ref, bf16[8,2,128,128]{3,2,1,0:T(8,128)(2,1)} %collective-permute-done.3.refs_0_, bf16[8,2,128,128]{3,2,1,0:T(8,128)(2,1)} %collective-permute-done.4.refs_1_, ...), custom_call_target="tpu_custom_call" | custom-call | flops 8589934592 | bytes 4194304 | tf_op jit(solution)/shard_map/pallas_call | solution.py:225
  117.5 0.0 all-to-all-done.3.refs_0_
  117.5 2.1 %collective-permute-done.9.refs_2_ = bf16[4,64,512]{2,1,0:T(8,128)(2,1)S(1)} collective-permute-done((bf16[4,64,512]{2,1,0:T(8,128)(2,1)}, bf16[4,64,512]{2,1,0:T(8,128)(2,1)S(1)}, u32[]{:S(2)}, u32[]{:S(2)}) %collective-permute-start.9) | collective-permute-done | bytes 262176 | tf_op jit(solution)/shard_map/ppermute | solution.py:342
  119.5 0.0 collective-permute-done.8.refs_4_
  119.5 1.5 %collective-permute-done.7.refs_1_ = bf16[8,64,512]{2,1,0:T(8,128)(2,1)} collective-permute-done((bf16[8,64,512]{2,1,0:T(8,128)(2,1)S(1)}, bf16[8,64,512]{2,1,0:T(8,128)(2,1)}, u32[]{:S(2)}, u32[]{:S(2)}) %collective-permute-start.7) | collective-permute-done | bytes 524320 | tf_op jit(solution)/shard_map/ppermute | solution.py:342
  121.0 6.8 %all-to-all-start.4 = ((bf16[8,128,256]{2,1,0:T(8,128)(2,1)}), bf16[8,128,256]{2,1,0:T(8,128)(2,1)S(1)}, u32[]{:S(2)}, u32[]{:S(2)}) async-start(bf16[8,128,256]{2,1,0:T(8,128)(2,1)} %shard_map.79), calls=%async_computation.4 | async-start | bytes 1048576 | tf_op jit(solution)/shard_map/all_to_all | solution.py:312
  127.9 0.6 collective-permute-start.10
  128.5 0.1 pad_add_fusion.place_ref
  128.5 7.3 %collective-permute-done.10.refs_3_ = bf16[4,64,512]{2,1,0:T(8,128)(2,1)S(1)} collective-permute-done((bf16[4,64,512]{2,1,0:T(8,128)(2,1)S(1)}, bf16[4,64,512]{2,1,0:T(8,128)(2,1)S(1)}, u32[]{:S(2)}, u32[]{:S(2)}) %collective-permute-start.10) | collective-permute-done | bytes 262176 | tf_op jit(solution)/shard_map/ppermute | solution.py:342
  135.9 0.0 copy-done.2
  135.9 1.0 copy-done.8
  136.9 3.6 %shard_map.82 = bf16[192,256]{1,0:T(8,128)(2,1)} custom-call(s32[3]{0:T(128)S(1)} %pad_add_fusion.place_ref, bf16[8,64,512]{2,1,0:T(8,128)(2,1)S(1)} %all-to-all-done.2.refs_0_, bf16[8,64,512]{2,1,0:T(8,128)(2,1)} %collective-permute-done.7.refs_1_, bf16[4,64,512]{2,1,0:T(8,128)(2,1)S(1)} %collective-permute-done.9.refs_2_, ...), custom_call_target="tpu_custom_call" | custom-call | flops 402653184 | bytes 4194304 | tf_op jit(solution)/shard_map/pallas_call | solution.py:293
  140.4 2.2 %all-to-all-done.4.refs_1_ = bf16[8,128,256]{2,1,0:T(8,128)(2,1)S(1)} async-done(((bf16[8,128,256]{2,1,0:T(8,128)(2,1)}), bf16[8,128,256]{2,1,0:T(8,128)(2,1)S(1)}, u32[]{:S(2)}, u32[]{:S(2)}) %all-to-all-start.4) | async-done | bytes 524320 | tf_op jit(solution)/shard_map/all_to_all | solution.py:312
  142.6 1.1 shard_map.83
  (20 shorter events, 0.1 us)
Async XLA Ops:
  0.6 10.5 %copy-start.1 = (bf16[1024,192]{0,1:T(8,128)(2,1)S(1)}, bf16[1024,192]{0,1:T(8,128)(2,1)}, u32[]{:S(2)}) copy-start(bf16[1024,192]{0,1:T(8,128)(2,1)} %param.11) | copy-start | bytes 1179652
  0.6 11.9 %copy-start.10 = (s32[8]{0:T(128)S(1)}, s32[8]{0:T(128)}, u32[]{:S(2)}) copy-start(s32[8]{0:T(128)} %pos_ref.1) | copy-start | bytes 100
  0.7 11.9 %copy-start = (bf16[128,4096]{1,0:T(8,128)(2,1)S(1)}, bf16[128,4096]{1,0:T(8,128)(2,1)}, u32[]{:S(2)}) copy-start(bf16[128,4096]{1,0:T(8,128)(2,1)} %q_ref.1) | copy-start | bytes 3145732
  2.7 26.0 %all-to-all-start = ((bf16[8,2,128,128]{3,2,1,0:T(8,128)(2,1)}), bf16[8,2,128,128]{3,2,1,0:T(8,128)(2,1)S(1)}, u32[]{:S(2)}, u32[]{:S(2)}) async-start(bf16[8,2,128,128]{3,2,1,0:T(8,128)(2,1)} %shard_map.77), calls=%async_computation | async-start | bytes 1048576 | tf_op jit(solution)/shard_map/all_to_all | solution.py:312
  11.2 3.3 %collective-permute-start.1 = (bf16[192,1024]{1,0:T(8,128)(2,1)S(1)}, bf16[192,1024]{1,0:T(8,128)(2,1)S(1)}, u32[]{:S(2)}, u32[]{:S(2)}) collective-permute-start(bf16[192,1024]{1,0:T(8,128)(2,1)S(1)} %bitcast.7), channel_id=1, source_target_pairs={{0,1},{1,0},{2,3},{3,2},{4,5},{5,4},{6,7},{7,6},{8,9},{9,8},{10,11... | collective-permute-start | bytes 1179656 | tf_op jit(solution)/shard_map/ppermute | solution.py:331
  11.3 11.5 %collective-permute-start = (bf16[192,1024]{1,0:T(8,128)(2,1)S(1)}, bf16[192,1024]{1,0:T(8,128)(2,1)S(1)}, u32[]{:S(2)}, u32[]{:S(2)}) collective-permute-start(bf16[192,1024]{1,0:T(8,128)(2,1)S(1)} %bitcast.8), channel_id=1, source_target_pairs={{0,2},{2,0},{1,3},{3,1},{4,6},{6,4},{5,7},{7,5},{8,10},{10,8},{9,1... | collective-permute-start | bytes 1179656 | tf_op jit(solution)/shard_map/ppermute | solution.py:330
  14.4 0.7 copy-start.3
  22.8 23.6 %copy-start.5 = (bf16[192,1024]{1,0:T(8,128)(2,1)}, bf16[192,1024]{1,0:T(8,128)(2,1)S(1)}, u32[]{:S(2)}) copy-start(bf16[192,1024]{1,0:T(8,128)(2,1)S(1)} %collective-permute-done.refs_8_) | copy-start | bytes 1179652
  28.6 35.5 %all-to-all-start.1 = ((bf16[8,144,512]{2,1,0:T(8,128)(2,1)}), bf16[8,144,512]{2,1,0:T(8,128)(2,1)S(1)}, u32[]{:S(2)}, u32[]{:S(2)}) async-start(bf16[8,144,512]{2,1,0:T(8,128)(2,1)} %shard_map.78), calls=%async_computation.1 | async-start | bytes 2359296 | tf_op jit(solution)/shard_map/all_to_all | solution.py:312
  32.2 32.0 %collective-permute-start.6 = (bf16[8,2,128,128]{3,2,1,0:T(8,128)(2,1)S(1)}, bf16[8,2,128,128]{3,2,1,0:T(8,128)(2,1)S(1)}, u32[]{:S(2)}, u32[]{:S(2)}) collective-permute-start(bf16[8,2,128,128]{3,2,1,0:T(8,128)(2,1)S(1)} %all-to-all-done.refs_4_), channel_id=1, source_target_pairs={{0,32},{32,64},{64,96},{96,1},{1,33},{33,65},{65,97},{97,2},{2,34}... | collective-permute-start | bytes 1572872 | tf_op jit(solution)/shard_map/ppermute | solution.py:319
  35.7 28.4 %collective-permute-start.5 = (bf16[8,2,128,128]{3,2,1,0:T(8,128)(2,1)S(1)}, bf16[8,2,128,128]{3,2,1,0:T(8,128)(2,1)}, u32[]{:S(2)}, u32[]{:S(2)}) collective-permute-start(bf16[8,2,128,128]{3,2,1,0:T(8,128)(2,1)S(1)} %all-to-all-done.refs_4_), channel_id=1, source_target_pairs={{0,96},{32,1},{64,33},{96,65},{1,97},{33,2},{65,34},{97,66},{2,98}... | collective-permute-start | bytes 1572872 | tf_op jit(solution)/shard_map/ppermute | solution.py:319
  39.9 24.3 %collective-permute-start.4 = (bf16[8,2,128,128]{3,2,1,0:T(8,128)(2,1)S(1)}, bf16[8,2,128,128]{3,2,1,0:T(8,128)(2,1)}, u32[]{:S(2)}, u32[]{:S(2)}) collective-permute-start(bf16[8,2,128,128]{3,2,1,0:T(8,128)(2,1)S(1)} %all-to-all-done.refs_4_), channel_id=1, source_target_pairs={{0,64},{32,96},{64,1},{96,33},{1,65},{33,97},{65,2},{97,34},{2,66}... | collective-permute-start | bytes 1572872 | tf_op jit(solution)/shard_map/ppermute | solution.py:319
  44.1 20.1 %collective-permute-start.3 = (bf16[8,2,128,128]{3,2,1,0:T(8,128)(2,1)S(1)}, bf16[8,2,128,128]{3,2,1,0:T(8,128)(2,1)}, u32[]{:S(2)}, u32[]{:S(2)}) collective-permute-start(bf16[8,2,128,128]{3,2,1,0:T(8,128)(2,1)S(1)} %all-to-all-done.refs_4_), channel_id=1, source_target_pairs={{0,1},{32,33},{64,65},{96,97},{1,2},{33,34},{65,66},{97,98},{2,3},... | collective-permute-start | bytes 1572872 | tf_op jit(solution)/shard_map/ppermute | solution.py:319
  46.4 1.7 %collective-permute-start.2 = (bf16[192,1024]{1,0:T(8,128)(2,1)S(1)}, bf16[192,1024]{1,0:T(8,128)(2,1)S(1)}, u32[]{:S(2)}, u32[]{:S(2)}) collective-permute-start(bf16[192,1024]{1,0:T(8,128)(2,1)S(1)} %collective-permute-done.refs_8_), channel_id=1, source_target_pairs={{0,1},{1,0},{2,3},{3,2},{4,5},{5,4},{6,7},{7,6},{8,9},{9,8},{10,11... | collective-permute-start | bytes 1179656 | tf_op jit(solution)/shard_map/ppermute | solution.py:333
  48.1 21.6 %copy-start.7 = (bf16[192,1024]{1,0:T(8,128)(2,1)}, bf16[192,1024]{1,0:T(8,128)(2,1)S(1)}, u32[]{:S(2)}) copy-start(bf16[192,1024]{1,0:T(8,128)(2,1)S(1)} %collective-permute-done.2.refs_9_) | copy-start | bytes 1179652
  64.2 10.8 %copy-start.11 = (bf16[8,2,128,128]{3,2,1,0:T(8,128)(2,1)}, bf16[8,2,128,128]{3,2,1,0:T(8,128)(2,1)S(1)}, u32[]{:S(2)}) copy-start(bf16[8,2,128,128]{3,2,1,0:T(8,128)(2,1)S(1)} %collective-permute-done.6.refs_3_) | copy-start | bytes 1572868
  69.7 22.8 %all-to-all-start.2 = ((bf16[8,64,512]{2,1,0:T(8,128)(2,1)}), bf16[8,64,512]{2,1,0:T(8,128)(2,1)S(1)}, u32[]{:S(2)}, u32[]{:S(2)}) async-start(bf16[8,64,512]{2,1,0:T(8,128)(2,1)} %shard_map.81), calls=%async_computation.2 | async-start | bytes 1048576 | tf_op jit(solution)/shard_map/all_to_all | solution.py:312
  92.5 25.0 %all-to-all-start.3 = ((bf16[8,128,256]{2,1,0:T(8,128)(2,1)}), bf16[8,128,256]{2,1,0:T(8,128)(2,1)S(1)}, u32[]{:S(2)}, u32[]{:S(2)}) async-start(bf16[8,128,256]{2,1,0:T(8,128)(2,1)} %shard_map.80), calls=%async_computation.3 | async-start | bytes 1048576 | tf_op jit(solution)/shard_map/all_to_all | solution.py:312
  97.3 22.3 %collective-permute-start.8 = (bf16[8,64,512]{2,1,0:T(8,128)(2,1)S(1)}, bf16[8,64,512]{2,1,0:T(8,128)(2,1)S(1)}, u32[]{:S(2)}, u32[]{:S(2)}) collective-permute-start(bf16[8,64,512]{2,1,0:T(8,128)(2,1)S(1)} %all-to-all-done.2.refs_0_), channel_id=1, source_target_pairs={{0,96},{32,0},{64,32},{96,64},{1,97},{33,1},{65,33},{97,65},{2,98}... | collective-permute-start | bytes 1572872 | tf_op jit(solution)/shard_map/ppermute | solution.py:342
  100.7 20.4 %collective-permute-start.7 = (bf16[8,64,512]{2,1,0:T(8,128)(2,1)S(1)}, bf16[8,64,512]{2,1,0:T(8,128)(2,1)}, u32[]{:S(2)}, u32[]{:S(2)}) collective-permute-start(bf16[8,64,512]{2,1,0:T(8,128)(2,1)S(1)} %all-to-all-done.2.refs_0_), channel_id=1, source_target_pairs={{0,32},{32,64},{64,96},{96,0},{1,33},{33,65},{65,97},{97,1},{2,34}... | collective-permute-start | bytes 1572872 | tf_op jit(solution)/shard_map/ppermute | solution.py:342
  100.7 18.9 %collective-permute-start.9 = (bf16[4,64,512]{2,1,0:T(8,128)(2,1)}, bf16[4,64,512]{2,1,0:T(8,128)(2,1)S(1)}, u32[]{:S(2)}, u32[]{:S(2)}) collective-permute-start(bf16[4,64,512]{2,1,0:T(8,128)(2,1)} %slice.6), channel_id=1, source_target_pairs={{0,64},{32,96},{64,0},{96,32},{1,65},{33,97},{65,1},{97,33},{2,66}... | collective-permute-start | bytes 786440 | tf_op jit(solution)/shard_map/ppermute | solution.py:342
  102.1 1.0 copy-start.12
  117.5 18.4 %copy-start.2 = (bf16[1024,192]{0,1:T(8,128)(2,1)S(1)}, bf16[1024,192]{0,1:T(8,128)(2,1)}, u32[]{:S(2)}) copy-start(bf16[1024,192]{0,1:T(8,128)(2,1)} %param.11) | copy-start | bytes 1179652
  117.5 18.4 %copy-start.4 = (bf16[192,1024]{1,0:T(8,128)(2,1)S(1)}, bf16[192,1024]{1,0:T(8,128)(2,1)}, u32[]{:S(2)}) copy-start(bf16[192,1024]{1,0:T(8,128)(2,1)} %copy-done.3) | copy-start | bytes 1179652
  117.5 18.4 %copy-start.6 = (bf16[192,1024]{1,0:T(8,128)(2,1)S(1)}, bf16[192,1024]{1,0:T(8,128)(2,1)}, u32[]{:S(2)}) copy-start(bf16[192,1024]{1,0:T(8,128)(2,1)} %copy-done.5) | copy-start | bytes 1179652
  117.5 18.4 %copy-start.9 = (f32[4096]{0:T(1024)S(1)}, f32[4096]{0:T(1024)}, u32[]{:S(2)}) copy-start(f32[4096]{0:T(1024)} %param.10) | copy-start | bytes 49156
  121.0 21.6 %all-to-all-start.4 = ((bf16[8,128,256]{2,1,0:T(8,128)(2,1)}), bf16[8,128,256]{2,1,0:T(8,128)(2,1)S(1)}, u32[]{:S(2)}, u32[]{:S(2)}) async-start(bf16[8,128,256]{2,1,0:T(8,128)(2,1)} %shard_map.79), calls=%async_computation.4 | async-start | bytes 1048576 | tf_op jit(solution)/shard_map/all_to_all | solution.py:312
  127.9 8.0 %collective-permute-start.10 = (bf16[4,64,512]{2,1,0:T(8,128)(2,1)S(1)}, bf16[4,64,512]{2,1,0:T(8,128)(2,1)S(1)}, u32[]{:S(2)}, u32[]{:S(2)}) collective-permute-start(bf16[4,64,512]{2,1,0:T(8,128)(2,1)S(1)} %slice.7), channel_id=1, source_target_pairs={{0,64},{32,96},{64,0},{96,32},{1,65},{33,97},{65,1},{97,33},{2,66}... | collective-permute-start | bytes 786440 | tf_op jit(solution)/shard_map/ppermute | solution.py:342
  135.9 1.0 copy-start.8
